TPU v7x, 128 devices: a whole 4x4x4 slice. The times are simulated.
128 devices in a mesh: row: 8 (over y, x_hi), col: 16 (over x_lo, z, core).
Axes of the slice: x: 4 (x_hi: 2, x_lo: 2; x = x_hi * 2 + x_lo), y: 4, z: 4, core: 2. Of those that a mesh axis runs over, the one named last changes fastest.
Arguments:
- coef_occ: bfloat16 [16384, 2560], P('row', 'col'), may hold values from -6 to 6
- coef_resp: bfloat16 [16384, 2560], P('col', 'row'), may hold values from -0.125 to 0.125
- orb_energy: float32 [2560], P('col'), may hold values from -2 to -0.3
- lap_index: int32 [1], replicated, may hold values from 0 to 7
- density_mask: int32 [128, 128], P('row', 'col'), may hold values 0 or 1
- tri_blocks: bfloat16 [8, 64, 128, 128], P('row'), may hold values from -0.5 to 0.5
- block_ao: int32 [8, 64], P('row'), may hold values from 0 to 15
- block_slab: int32 [8, 64], P('row'), may hold values from 0 to 15
- metric: bfloat16 [2048, 128], P('col'), may hold values from -0.1875 to 0.1875
Outputs:
- pseudo: bfloat16 [16384, 16384], P('row', 'col')
- ri_grad: bfloat16 [16384, 2048], P('row', 'col')
All inputs are finite; a program needn't handle non-finite values. No bound on the sum of `density_mask` on one device may be relied on, other than what follows from the above.
Results may differ from a plain program's by a relative error of at most 0.014.
Values may be sent and summed in bfloat16 or wider, within the bound.
No kernel may reach another device: no remote copies, remote signals or barrier semaphores. Data moves between devices by JAX's collectives and lax.ppermute only.
A program may use at most 192 MiB of HBM per device.

v0:
```python
import math

import jax
import jax.numpy as jnp
from jax import lax
from jax.sharding import PartitionSpec as P


def shards(
    coef_occ,
    coef_resp,
    orb_energy,
    lap_index,
    density_mask,
    tri_blocks,
    block_ao,
    block_slab,
    metric,
):
    t_point = 0.04 * jnp.exp(0.5 * math.log(2.0) * lap_index[0].astype(jnp.float32))
    weighted = (coef_occ.astype(jnp.float32) * jnp.exp(t_point * orb_energy)[None, :]).astype(
        jnp.bfloat16
    )
    rows_here = coef_occ.shape[0]
    cols_here = coef_resp.shape[0]
    contract = (((1,), (1,)), ((), ()))
    resp_whole = lax.all_gather(coef_resp, "row", axis=1, tiled=True)
    product = lax.dot_general(
        lax.all_gather(weighted, "col", axis=1, tiled=True),
        resp_whole,
        contract,
        preferred_element_type=jnp.float32,
    )
    mask_rows, mask_cols = density_mask.shape
    masked = (
        product.reshape(mask_rows, 128, mask_cols, 128)
        * density_mask.astype(jnp.float32)[:, None, :, None]
    )
    pseudo = masked.reshape(rows_here, cols_here).astype(jnp.bfloat16)
    slab_count = lax.axis_size("col")
    picked = pseudo.reshape(rows_here // 128, 128, cols_here)[block_ao[0]]
    partial_value = jnp.einsum(
        "bmq,bmc->bqc", tri_blocks[0], picked, preferred_element_type=jnp.float32
    )
    slab_sum = jax.ops.segment_sum(partial_value, block_slab[0], num_segments=slab_count).astype(
        jnp.bfloat16
    )
    ri_width = slab_sum.shape[1]
    received = lax.all_to_all(slab_sum, "col", split_axis=0, concat_axis=0, tiled=True)
    gamma_t = jnp.transpose(received, (0, 2, 1)).reshape(-1, ri_width)
    grad = lax.psum_scatter(
        lax.dot_general(gamma_t, metric, contract, preferred_element_type=jnp.float32),
        "row",
        scatter_dimension=0,
        tiled=True,
    )
    return (pseudo, grad.astype(jnp.bfloat16))


def solution(mesh):
    placed = (
        P("row", "col"),
        P("col", "row"),
        P("col"),
        P(),
        P("row", "col"),
        P("row", None, None, None),
        P("row", None),
        P("row", None),
        P("col", None),
    )
    return jax.shard_map(
        shards,
        mesh=mesh,
        in_specs=placed,
        out_specs=(P("row", "col"), P("row", "col")),
        check_vma=False,
    )
```

profile of v0, /device:TPU:103, one launch (start us, length us, event | category | flops | bytes accessed | tf_op | source)
XLA Modules:
  0.0 500.7 jit_solution(2809777048132648972)
XLA Ops:
  7.2 0.7 all-gather.5.cloned.1.call-update
  7.9 0.0 all-gather.3.cloned.1.call-start
  8.6 0.7 multiply_exponential_fusion
  9.3 2.1 multiply_convert_fusion
  11.5 0.0 reduce-scatter.2.cloned.1.call-start
  11.5 0.7 convert_element_type.25
  12.2 0.1 copy.13
  12.3 0.7 fusion.2
  12.9 76.7 %all-gather.5.cloned.1.call-done = bf16[1024,2560]{0,1:T(8,128)(2,1)} async-done(((bf16[1024,320]{0,1:T(8,128)(2,1)}), bf16[1024,2560]{0,1:T(8,128)(2,1)}) %all-gather.5.cloned.1.call-update) | async-done | bytes 5242896 | tf_op jit(solution)/shard_map/all_gather | solution.py:27
  89.7 63.8 %all-gather.3.cloned.1.call-done = bf16[2048,2560]{0,1:T(8,128)(2,1)} async-done(((bf16[2048,160]{0,1:T(8,128)(2,1)}), bf16[2048,2560]{0,1:T(8,128)(2,1)}) %all-gather.3.cloned.1.call-update) | async-done | bytes 10485776 | tf_op jit(solution)/shard_map/all_gather | solution.py:29
  153.5 0.6 mul.29
  154.1 1.9 copy-done.4
  156.0 16.0 %fusion = bf16[2048,1024]{1,0:T(8,128)(2,1)} fusion(f32[256,8,8,128]{3,2,1,0:T(8,128)S(1)} %bitcast.28, bf16[2048,2560]{0,1:T(8,128)(2,1)} %all-gather.3.cloned.1.call-done, bf16[1024,2560]{0,1:T(8,128)(2,1)S(1)} %copy-done.4), kind=kOutput, calls=%fused_computation.4 | convolution fusion | flops 10741612544 | bytes 28311552 | tf_op jit(solution)/shard_map/dot_general | solution.py:28
  172.0 9.8 %gather_fusion = bf16[64,128,1024]{2,1,0:T(8,128)(2,1)} fusion(bf16[16,128,1024]{2,1,0:T(8,128)(2,1)} %bitcast.25, s32[1024]{0:T(1024)S(1)} %pad_clamp_fusion), kind=kCustom, calls=%fused_computation | custom fusion | bytes 33554688 | tf_op jit(solution)/shard_map/gather | solution.py:41
  181.8 17.7 %convolution_bitcast_fusion = f32[64,128,1024]{1,2,0:T(8,128)} fusion(bf16[64,128,1024]{2,1,0:T(8,128)(2,1)} %gather_fusion, bf16[1,64,128,128]{3,2,1,0:T(8,128)(2,1)S(1)} %copy-done), kind=kOutput, calls=%fused_computation.2 | convolution fusion | flops 2147483648 | bytes 52428800 | tf_op jit(solution)/shard_map/bmq,bmc->bqc/dot_general | solution.py:42
  199.5 33.4 %copy.15 = f32[64,128,1024]{2,1,0:T(8,128)} copy(f32[64,128,1024]{1,2,0:T(8,128)} %convolution_bitcast_fusion) | data formatting | bytes 67108864 | tf_op jit(solution)/shard_map/bmq,bmc->bqc/dot_general | solution.py:42
  232.9 4.3 broadcast_in_dim.2
  237.2 70.5 %scatter_fusion = f32[16,128,1024]{2,1,0:T(8,128)} fusion(f32[16,128,1024]{2,1,0:T(8,128)} %broadcast_in_dim.2, s32[64]{0:T(128)S(1)} %bitcast.29, f32[64,128,1024]{2,1,0:T(8,128)} %copy.15), kind=kCustom, calls=%fused_computation.1 | custom fusion | flops 8388608 | bytes 100663552 | tf_op jit(solution)/shard_map/scatter-add | solution.py:45
  307.7 4.0 convert_element_type.27
  311.8 53.3 %all_to_all.5 = bf16[16,128,1024]{2,1,0:T(8,128)(2,1)} all-to-all(bf16[16,128,1024]{2,1,0:T(8,128)(2,1)S(1)} %convert_element_type.27), channel_id=1, replica_groups=mesh['row'=8,'col'=16] {'col'}, dimensions={0} | all-to-all | bytes 8388608 | tf_op jit(solution)/shard_map/all_to_all | solution.py:49
  365.1 6.3 %copy.16 = bf16[16,1024,128]{2,1,0:T(8,128)(2,1)} copy(bf16[16,1024,128]{1,2,0:T(8,128)(2,1)} %bitcast.27) | data formatting | bytes 8388608 | tf_op jit(solution)/shard_map/transpose | solution.py:50
  371.4 6.8 %fusion.3 = f32[16384,128]{1,0:T(8,128)} fusion(bf16[16384,128]{1,0:T(8,128)(2,1)} %bitcast.26, bf16[128,128]{1,0:T(8,128)(2,1)S(1)} %copy-done.2), kind=kOutput, calls=%fused_computation.11 | convolution fusion | flops 536870912 | bytes 12615680 | tf_op jit(solution)/shard_map/dot_general | solution.py:52
  378.2 113.8 %reduce-scatter.2.cloned.1.call-done = f32[2048,128]{1,0:T(8,128)} async-done(((f32[16384,128]{1,0:T(8,128)}), f32[2048,128]{1,0:T(8,128)}) %reduce-scatter.2.cloned.1.call-update) | async-done | bytes 1048592 | tf_op jit(solution)/shard_map/reduce_scatter | solution.py:51
  492.1 2.1 convert_element_type.28
  (13 shorter events, 0.1 us)
Async XLA Ops:
  7.2 174.6 %copy-start = (bf16[1,64,128,128]{3,2,1,0:T(8,128)(2,1)S(1)}, bf16[1,64,128,128]{3,2,1,0:T(8,128)(2,1)}, u32[]{:S(2)}) copy-start(bf16[1,64,128,128]{3,2,1,0:T(8,128)(2,1)} %param.14) | copy-start | bytes 6291460
  7.2 82.5 %all-gather.5.cloned.1.call-start = ((), (), s32[]{:S(2)}) async-start(), calls=%async_computation.3 | async-start | bytes 5898240 | tf_op jit(solution)/shard_map/all_gather | solution.py:27
  7.9 145.6 %all-gather.3.cloned.1.call-start = ((), (), s32[]{:S(2)}) async-start(), calls=%async_computation.2 | async-start | bytes 11141120 | tf_op jit(solution)/shard_map/all_gather | solution.py:29
  11.5 480.6 %reduce-scatter.2.cloned.1.call-start = ((), (), s32[]{:S(2)}) async-start(), calls=%async_computation.4 | async-start | bytes 9437184 | tf_op jit(solution)/shard_map/reduce_scatter | solution.py:51
  153.5 2.5 copy-start.4
  232.9 4.3 copy-start.3
  311.8 59.6 %copy-start.2 = (bf16[128,128]{1,0:T(8,128)(2,1)S(1)}, bf16[128,128]{1,0:T(8,128)(2,1)}, u32[]{:S(2)}) copy-start(bf16[128,128]{1,0:T(8,128)(2,1)} %param.17) | copy-start | bytes 98308
  371.4 122.8 %copy-start.1 = (bf16[1,64,128,128]{3,2,1,0:T(8,128)(2,1)S(1)}, bf16[1,64,128,128]{3,2,1,0:T(8,128)(2,1)}, u32[]{:S(2)}) copy-start(bf16[1,64,128,128]{3,2,1,0:T(8,128)(2,1)} %param.14) | copy-start | bytes 6291460
Sparse Core Ops, SparseCore 0:
  10.3 79.3 all-gather.4
  92.0 61.4 all-gather.2
  378.4 113.6 reduce-scatter.1
where the time goes:
time: 505 us; the launch traced here: 501 us
  waiting for transfers between devices  255 us (50%)
  other arithmetic  80.8 us (16%)
  local copies, waits for them, and re-layouts  56.4 us (11%)
  blocking collectives  53.3 us (11%)
  matrix products  40.5 us (8%)
  between operations  14.5 us (3%)
    reduce_scatter x1, waiting for transfers between devices, shards(): lax.psum_scatter(lax.dot_general(gamma_t, metric, contract, preferred_ele...  114 us
    all_gather x1, waiting for transfers between devices, shards(): resp_whole = lax.all_gather(coef_resp, 'row', axis=1, tiled=True)  76.7 us
    scatter-add x1, other arithmetic, shards(): jax.ops.segment_sum(partial_value, block_slab[0], num_segments=slab_count)  70.5 us
    all_gather x1, waiting for transfers between devices, shards(): lax.all_gather(weighted, 'col', axis=1, tiled=True)  63.8 us
    all_to_all x1, blocking collectives, shards(): lax.all_to_all(slab_sum, 'col', split_axis=0, concat_axis=0, tiled=True)  53.3 us
    dot_general x1, local copies, waits for them, and re-layouts, shards(): jnp.einsum('bmq,bmc->bqc', tri_blocks[0], picked, preferred_element_type=...  33.4 us
    dot_general x1, matrix products, shards(): jnp.einsum('bmq,bmc->bqc', tri_blocks[0], picked, preferred_element_type=...  17.7 us
    dot_general x1, matrix products, shards(): lax.dot_general(lax.all_gather(weighted, 'col', axis=1, tiled=True), resp...  16 us
  transfers between devices with their start and end apart: 3, of which 3 were waited for; matrix products, arithmetic and copies ran while one was open for 1% of the time, Pallas kernels for 0%

commit v1 on v0

v1 whole, which is shorter than its diff:
```python
import functools
import math

import jax
import jax.numpy as jnp
from jax import lax
from jax.experimental import pallas as pl
from jax.experimental.pallas import tpu as pltpu
from jax.sharding import PartitionSpec as P

N_ROW = 8
N_COL = 16
BOTH = ("row", "col")


def send(x, to):
    pairs = []
    for r in range(N_ROW):
        for c in range(N_COL):
            rr, cc = to(r, c)
            pairs.append((r * N_COL + c, rr * N_COL + cc))
    return lax.ppermute(x, BOTH, pairs)


def along_y(step):
    return lambda r, c: ((r + 2 * step) % N_ROW, c)


def flip_x(r, c):
    return r ^ 1, c


def owner_of(j):
    return lambda r, c: (c // 2, (r // 2) * 4 + ((2 * (r % 2) + c % 2) ^ j))


def slab_kernel(first, ao, slab_at, tri_ref, pseudo_ref, *outs):
    for k in range(4):
        for j in range(4):
            s = slab_at[4 * k + j]

            def add(p, total):
                rhs = jnp.concatenate(
                    [
                        pseudo_ref[pl.ds(pl.multiple_of(ao[2 * p + h] * 128, 128), 128), :]
                        for h in range(2)
                    ],
                    axis=0,
                )
                return total + jnp.dot(tri_ref[p], rhs, preferred_element_type=jnp.float32)

            total = lax.fori_loop(
                first[s], first[s + 1], add, jnp.zeros((128, pseudo_ref.shape[1]), jnp.float32)
            )
            outs[k][j] = total.astype(jnp.bfloat16)


def slab_sums(first, ao, slab_at, tri_pairs, pseudo):
    cols = pseudo.shape[1]
    piece = jax.ShapeDtypeStruct((4, 128, cols), jnp.bfloat16)
    return pl.pallas_call(
        slab_kernel,
        grid_spec=pltpu.PrefetchScalarGridSpec(
            num_scalar_prefetch=3,
            grid=(1,),
            in_specs=[
                pl.BlockSpec(tri_pairs.shape, lambda i, *_: (0, 0, 0)),
                pl.BlockSpec(pseudo.shape, lambda i, *_: (0, 0)),
            ],
            out_specs=[pl.BlockSpec((4, 128, cols), lambda i, *_: (0, 0, 0))] * 4,
        ),
        out_shape=[piece] * 4,
        compiler_params=pltpu.CompilerParams(vmem_limit_bytes=48 * 1024 * 1024),
        cost_estimate=pl.CostEstimate(
            flops=2 * 40 * 128 * 256 * cols, bytes_accessed=12 * 1024 * 1024, transcendentals=0
        ),
    )(first, ao, slab_at, tri_pairs, pseudo)


def shards(
    coef_occ,
    coef_resp,
    orb_energy,
    lap_index,
    density_mask,
    tri_blocks,
    block_ao,
    block_slab,
    metric,
):
    row, col = lax.axis_index("row"), lax.axis_index("col")
    y, x, core = row // 2, row % 2, col % 2
    t_point = 0.04 * jnp.exp(0.5 * math.log(2.0) * lap_index[0].astype(jnp.float32))
    weighted = (coef_occ.astype(jnp.float32) * jnp.exp(t_point * orb_energy)[None, :]).astype(
        jnp.bfloat16
    )
    w_all = lax.all_gather(weighted.T, "col", axis=0, tiled=True)

    mine = coef_resp.T
    other = send(mine, flip_x)
    depth = mine.shape[0]
    r_all = jnp.zeros((N_ROW * depth, mine.shape[1]), mine.dtype)

    def place(r_all, part, step, xx):
        at = (((y + 4 - step) % 4) * 2 + xx) * depth
        return lax.dynamic_update_slice(r_all, part, (at, 0))

    r_all = place(r_all, mine, 0, x)
    for step in (1, 3, 2):
        r_all = place(r_all, send(mine, along_y(step)), step, x)
    r_all = place(r_all, other, 0, 1 - x)
    for step in (1, 3, 2):
        r_all = place(r_all, send(other, along_y(step)), step, 1 - x)

    ao, slab = block_ao[0], block_slab[0]
    n_blocks = slab.shape[0]
    n_pairs = n_blocks // 2 + N_COL
    ids = jnp.arange(n_blocks, dtype=jnp.int32)
    rank = jnp.sum(
        ((slab[None, :] == slab[:, None]) & (ids[None, :] < ids[:, None])).astype(jnp.int32), axis=1
    )
    slabs = jnp.arange(N_COL + 1, dtype=jnp.int32)
    counts = jnp.sum((slab[None, :] == slabs[:N_COL, None]).astype(jnp.int32), axis=1)
    pairs = (counts + 1) // 2
    first = jnp.sum(jnp.where(slabs[None, :N_COL] < slabs[:, None], pairs[None, :], 0), axis=1)
    start = jnp.sum(jnp.where(slabs[None, :N_COL] < slab[:, None], pairs[None, :], 0), axis=1)
    slot = 2 * start + rank
    hit = jnp.arange(2 * n_pairs, dtype=jnp.int32)[:, None] == slot[None, :]
    block_in = jnp.sum(jnp.where(hit, ids[None, :], 0), axis=1)
    ao_in = jnp.sum(jnp.where(hit, ao[None, :], 0), axis=1)
    used = jnp.any(hit, axis=1)
    tri_in = jnp.where(used[:, None, None], tri_blocks[0][block_in], 0)
    tri_pairs = tri_in.reshape(n_pairs, 256, 128).transpose(0, 2, 1)
    order = [
        ((y + k) % 4) * 4 + ((2 * x + core) ^ j) for k in range(4) for j in range(4)
    ]
    slab_at = jnp.stack(order).astype(jnp.int32)

    rows_here = coef_occ.shape[0]
    cols_here = coef_resp.shape[0]
    product = lax.dot_general(
        w_all, r_all, (((0,), (0,)), ((), ())), preferred_element_type=jnp.float32
    )
    mask_rows, mask_cols = density_mask.shape
    masked = (
        product.reshape(mask_rows, 128, mask_cols, 128)
        * density_mask.astype(jnp.float32)[:, None, :, None]
    )
    pseudo = masked.reshape(rows_here, cols_here).astype(jnp.bfloat16)

    pieces = slab_sums(first, ao_in, slab_at, tri_pairs, pseudo)
    total = pieces[0].astype(jnp.float32)
    arrived = [send(pieces[k], along_y(k)) for k in (1, 3, 2)]
    for part in arrived:
        total = total + part.astype(jnp.float32)
    total = total.astype(jnp.bfloat16)
    got = [send(total[j], owner_of(j)) for j in range(4)]
    i = col % 4
    first_half, second_half = [], []
    for j in range(4):
        e = (i ^ j) % 2
        first_half.append(jnp.where(e == 0, got[j], 0).astype(jnp.float32))
        second_half.append(jnp.where(e == 1, got[j], 0).astype(jnp.float32))
    whole = jnp.concatenate([sum(first_half), sum(second_half)], axis=1).astype(jnp.bfloat16)
    grad = lax.dot_general(
        whole, metric, (((0,), (1,)), ((), ())), preferred_element_type=jnp.float32
    )
    return (pseudo, grad.astype(jnp.bfloat16))


def solution(mesh):
    placed = (
        P("row", "col"),
        P("col", "row"),
        P("col"),
        P(),
        P("row", "col"),
        P("row", None, None, None),
        P("row", None),
        P("row", None),
        P("col", None),
    )
    return jax.shard_map(
        shards,
        mesh=mesh,
        in_specs=placed,
        out_specs=(P("row", "col"), P("row", "col")),
        check_vma=False,
    )
```

time: 505 us -> 273 us (0.54)
  the two profiles are of different devices: /device:TPU:103 before, /device:TPU:67 now
where the time goes in v1:
time: 273 us
  waiting for transfers between devices  159 us (58%)
  starting transfers between devices  28.7 us (11%)
  local copies, waits for them, and re-layouts  25 us (9%)
  matrix products  17.1 us (6%)
  Pallas kernels  15.7 us (6%)
  between operations  15.2 us (6%)
  other arithmetic  11.5 us (4%)
    ppermute x14, waiting for transfers between devices, send(): return lax.ppermute(x, BOTH, pairs)  149 us
    ppermute x14, starting transfers between devices, send(): return lax.ppermute(x, BOTH, pairs)  28.6 us
    dot_general x1, matrix products, shards(): lax.dot_general(w_all, r_all, (((0,), (0,)), ((), ())), preferred_element...  16 us
    pallas_call x1, Pallas kernels, slab_sums(): pl.pallas_call(slab_kernel, grid_spec=pltpu.PrefetchScalarGridSpec(num_sc...  15.7 us
    dynamic_update_slice x8, local copies, waits for them, and re-layouts, place(): return lax.dynamic_update_slice(r_all, part, (at, 0))  10.7 us
    all_gather x1, waiting for transfers between devices, shards(): w_all = lax.all_gather(weighted.T, 'col', axis=0, tiled=True)  10.2 us
    gather x2, local copies, waits for them, and re-layouts, shards(): tri_in = jnp.where(used[:, None, None], tri_blocks[0][block_in], 0)  7.42 us
  transfers between devices with their start and end apart: 15, of which 10 were waited for; matrix products, arithmetic and copies ran while one was open for 10% of the time, Pallas kernels for 0%

profile of v1, /device:TPU:67, one launch (start us, length us, event | category | flops | bytes accessed | tf_op | source)
XLA Modules:
  0.0 272.7 jit_solution(16226250408251653400)
XLA Ops:
  8.7 2.1 fusion.1
  20.5 2.7 gather_fusion
  23.2 4.7 %copy.15 = bf16[48,256,128]{1,2,0:T(8,128)(2,1)} copy(bf16[48,256,128]{2,1,0:T(8,128)(2,1)} %bitcast.54) | data formatting | bytes 6291456 | tf_op jit(solution)/shard_map/gather | solution.py:132
  28.3 3.9 %select_bitcast_fusion.tri_ref = bf16[48,128,256]{2,1,0:T(8,128)(2,1)} fusion(bf16[48,256,128]{1,2,0:T(8,128)(2,1)} %copy.15, pred[48,256]{1,0:T(8,128)(4,1)S(1)} %bitcast.61), kind=kLoop, calls=%fused_computation.3 | loop fusion | flops 1572864 | bytes 6303744 | tf_op jit(solution)/shard_map/transpose | solution.py:133
  33.4 2.3 copy-done.1
  35.8 2.3 collective-permute-start.5
  38.8 2.0 constant_dynamic-update-slice_fusion.6
  43.4 2.0 constant_dynamic-update-slice_fusion.4
  46.3 13.2 %collective-permute-done.4 = bf16[320,1024]{1,0:T(8,128)(2,1)} collective-permute-done((bf16[320,1024]{1,0:T(8,128)(2,1)S(1)}, bf16[320,1024]{1,0:T(8,128)(2,1)}, u32[]{:S(2)}, u32[]{:S(2)}) %collective-permute-start.4) | collective-permute-done | bytes 655392 | tf_op jit(solution)/shard_map/ppermute | solution.py:22
  59.5 2.0 constant_dynamic-update-slice_fusion.2
  62.4 9.0 %collective-permute-done.6 = bf16[320,1024]{1,0:T(8,128)(2,1)S(1)} collective-permute-done((bf16[320,1024]{1,0:T(8,128)(2,1)S(1)}, bf16[320,1024]{1,0:T(8,128)(2,1)S(1)}, u32[]{:S(2)}, u32[]{:S(2)}) %collective-permute-start.6) | collective-permute-done | bytes 655392 | tf_op jit(solution)/shard_map/ppermute | solution.py:22
  72.3 10.2 %all-gather.2.cloned.1.call-done = bf16[2560,2048]{1,0:T(8,128)(2,1)} async-done(((bf16[160,2048]{1,0:T(8,128)(2,1)}), bf16[2560,2048]{1,0:T(8,128)(2,1)}) %all-gather.2.cloned.1.call-update) | async-done | bytes 10485776 | tf_op jit(solution)/shard_map/all_gather | solution.py:97
  85.0 16.0 %fusion.pseudo_ref = bf16[2048,1024]{1,0:T(8,128)(2,1)} fusion(f32[256,8,8,128]{3,2,1,0:T(8,128)S(1)} %bitcast.55, bf16[2560,2048]{1,0:T(8,128)(2,1)} %all-gather.2.cloned.1.call-done, bf16[2560,1024]{1,0:T(8,128)(2,1)S(1)} %copy-done.2), kind=kOutput, calls=%fused_computation.2 | convolution fusion | flops 10741612544 | bytes 28311552 | tf_op jit(solution)/shard_map/dot_general | solution.py:141
  101.0 15.7 %shard_map.104 = (bf16[4,128,1024]{2,1,0:T(8,128)(2,1)S(1)}, bf16[4,128,1024]{2,1,0:T(8,128)(2,1)S(1)}, bf16[4,128,1024]{2,1,0:T(8,128)(2,1)S(1)}, bf16[4,128,1024]{2,1,0:T(8,128)(2,1)S(1)}) custom-call(s32[17]{0:T(128)S(1)} %select_reduce_fusion.3.first, s32[96]{0:T(128)S(1)} %get-tuple-element.11.ao, s32[16]{0:T(128)S(1)} %stack.67.slab_at, ...), custom_call_target="tpu_custom_call" | custom-call | flops 2684354560 | bytes 12582912 | tf_op jit(solution)/shard_map/pallas_call | solution.py:61
  116.8 2.7 collective-permute-start.8
  119.7 23.5 %collective-permute-done.7 = bf16[4,128,1024]{2,1,0:T(8,128)(2,1)S(1)} collective-permute-done((bf16[4,128,1024]{2,1,0:T(8,128)(2,1)S(1)}, bf16[4,128,1024]{2,1,0:T(8,128)(2,1)S(1)}, u32[]{:S(2)}, u32[]{:S(2)}) %collective-permute-start.7) | collective-permute-done | bytes 1048608 | tf_op jit(solution)/shard_map/ppermute | solution.py:22
  143.2 21.1 %collective-permute-done.9 = bf16[4,128,1024]{2,1,0:T(8,128)(2,1)S(1)} collective-permute-done((bf16[4,128,1024]{2,1,0:T(8,128)(2,1)S(1)}, bf16[4,128,1024]{2,1,0:T(8,128)(2,1)S(1)}, u32[]{:S(2)}, u32[]{:S(2)}) %collective-permute-start.9) | collective-permute-done | bytes 1048608 | tf_op jit(solution)/shard_map/ppermute | solution.py:22
  166.1 6.3 %collective-permute-start.10 = (bf16[128,1024]{1,0:T(8,128)(2,1)}, bf16[128,1024]{1,0:T(8,128)(2,1)S(1)}, u32[]{:S(2)}, u32[]{:S(2)}) collective-permute-start(bf16[128,1024]{1,0:T(8,128)(2,1)} %get-tuple-element.14), channel_id=1, source_target_pairs={{0,0},{1,1},{2,16},{3,17},{4,32},{5,33},{6,48},{7,49},{8,64},{9,65... | collective-permute-start | bytes 786440 | tf_op jit(solution)/shard_map/ppermute | solution.py:22
  172.5 3.5 %collective-permute-start.11 = (bf16[128,1024]{1,0:T(8,128)(2,1)}, bf16[128,1024]{1,0:T(8,128)(2,1)S(1)}, u32[]{:S(2)}, u32[]{:S(2)}) collective-permute-start(bf16[128,1024]{1,0:T(8,128)(2,1)} %get-tuple-element.17), channel_id=1, source_target_pairs={{0,1},{1,0},{2,17},{3,16},{4,33},{5,32},{6,49},{7,48},{8,65},{9,64... | collective-permute-start | bytes 786440 | tf_op jit(solution)/shard_map/ppermute | solution.py:22
  176.5 6.1 %collective-permute-start.13 = (bf16[128,1024]{1,0:T(8,128)(2,1)S(1)}, bf16[128,1024]{1,0:T(8,128)(2,1)S(1)}, u32[]{:S(2)}, u32[]{:S(2)}) collective-permute-start(bf16[128,1024]{1,0:T(8,128)(2,1)S(1)} %get-tuple-element.15), channel_id=1, source_target_pairs={{0,3},{1,2},{2,19},{3,18},{4,35},{5,34},{6,51},{7,50},{8,67},{9,66... | collective-permute-start | bytes 786440 | tf_op jit(solution)/shard_map/ppermute | solution.py:22
  182.5 2.7 collective-permute-done.10
  185.2 23.4 %collective-permute-done.11 = bf16[128,1024]{1,0:T(8,128)(2,1)S(1)} collective-permute-done((bf16[128,1024]{1,0:T(8,128)(2,1)}, bf16[128,1024]{1,0:T(8,128)(2,1)S(1)}, u32[]{:S(2)}, u32[]{:S(2)}) %collective-permute-start.11) | collective-permute-done | bytes 262176 | tf_op jit(solution)/shard_map/ppermute | solution.py:22
  208.7 46.5 %collective-permute-done.12 = bf16[128,1024]{1,0:T(8,128)(2,1)S(1)} collective-permute-done((bf16[128,1024]{1,0:T(8,128)(2,1)}, bf16[128,1024]{1,0:T(8,128)(2,1)S(1)}, u32[]{:S(2)}, u32[]{:S(2)}) %collective-permute-start.12) | collective-permute-done | bytes 262176 | tf_op jit(solution)/shard_map/ppermute | solution.py:22
  255.1 9.2 %collective-permute-done.13 = bf16[128,1024]{1,0:T(8,128)(2,1)S(1)} collective-permute-done((bf16[128,1024]{1,0:T(8,128)(2,1)S(1)}, bf16[128,1024]{1,0:T(8,128)(2,1)S(1)}, u32[]{:S(2)}, u32[]{:S(2)}) %collective-permute-start.13) | collective-permute-done | bytes 262176 | tf_op jit(solution)/shard_map/ppermute | solution.py:22
  (57 shorter events, 24.2 us)
Async XLA Ops:
  7.2 13.3 %copy-start = (bf16[1,64,128,128]{3,2,1,0:T(8,128)(2,1)S(1)}, bf16[1,64,128,128]{3,2,1,0:T(8,128)(2,1)}, u32[]{:S(2)}) copy-start(bf16[1,64,128,128]{3,2,1,0:T(8,128)(2,1)} %param.14) | copy-start | bytes 6291460
  7.2 75.3 %all-gather.2.cloned.1.call-start = ((), (), s32[]{:S(2)}) async-start(), calls=%async_computation | async-start | bytes 11141120 | tf_op jit(solution)/shard_map/all_gather | solution.py:97
  10.9 27.6 %collective-permute-start = (bf16[320,1024]{1,0:T(8,128)(2,1)}, bf16[320,1024]{1,0:T(8,128)(2,1)}, u32[]{:S(2)}, u32[]{:S(2)}) collective-permute-start(bf16[320,1024]{1,0:T(8,128)(2,1)} %bitcast.56), channel_id=1, source_target_pairs={{0,32},{1,33},{2,34},{3,35},{4,36},{5,37},{6,38},{7,39},{8,40},{9,... | collective-permute-start | bytes 1966088 | tf_op jit(solution)/shard_map/ppermute | solution.py:22
  12.3 28.5 %collective-permute-start.1 = (bf16[320,1024]{1,0:T(8,128)(2,1)}, bf16[320,1024]{1,0:T(8,128)(2,1)}, u32[]{:S(2)}, u32[]{:S(2)}) collective-permute-start(bf16[320,1024]{1,0:T(8,128)(2,1)} %bitcast.57), channel_id=1, source_target_pairs={{0,96},{1,97},{2,98},{3,99},{4,100},{5,101},{6,102},{7,103},{8,104... | collective-permute-start | bytes 1966088 | tf_op jit(solution)/shard_map/ppermute | solution.py:22
  13.8 29.6 %collective-permute-start.2 = (bf16[320,1024]{1,0:T(8,128)(2,1)}, bf16[320,1024]{1,0:T(8,128)(2,1)}, u32[]{:S(2)}, u32[]{:S(2)}) collective-permute-start(bf16[320,1024]{1,0:T(8,128)(2,1)} %bitcast.58), channel_id=1, source_target_pairs={{0,64},{1,65},{2,66},{3,67},{4,68},{5,69},{6,70},{7,71},{8,72},{9,... | collective-permute-start | bytes 1966088 | tf_op jit(solution)/shard_map/ppermute | solution.py:22
  15.3 16.9 %collective-permute-start.3 = (bf16[320,1024]{1,0:T(8,128)(2,1)}, bf16[320,1024]{1,0:T(8,128)(2,1)S(1)}, u32[]{:S(2)}, u32[]{:S(2)}) collective-permute-start(bf16[320,1024]{1,0:T(8,128)(2,1)} %bitcast.59), channel_id=1, source_target_pairs={{0,16},{1,17},{2,18},{3,19},{4,20},{5,21},{6,22},{7,23},{8,24},{9,... | collective-permute-start | bytes 1966088 | tf_op jit(solution)/shard_map/ppermute | solution.py:22
  28.3 5.0 %copy-start.3 = (bf16[1024,320]{0,1:T(8,128)(2,1)S(1)}, bf16[1024,320]{0,1:T(8,128)(2,1)}, u32[]{:S(2)}) copy-start(bf16[1024,320]{0,1:T(8,128)(2,1)} %param.10) | copy-start | bytes 1966084
  28.3 9.9 %copy-start.5 = (s32[16,8]{0,1:T(8,128)S(1)}, s32[16,8]{0,1:T(8,128)}, u32[]{:S(2)}) copy-start(s32[16,8]{0,1:T(8,128)} %param.13) | copy-start | bytes 1540
  32.3 27.2 %collective-permute-start.4 = (bf16[320,1024]{1,0:T(8,128)(2,1)S(1)}, bf16[320,1024]{1,0:T(8,128)(2,1)}, u32[]{:S(2)}, u32[]{:S(2)}) collective-permute-start(bf16[320,1024]{1,0:T(8,128)(2,1)S(1)} %collective-permute-done.3), channel_id=1, source_target_pairs={{0,32},{1,33},{2,34},{3,35},{4,36},{5,37},{6,38},{7,39},{8,40},{9,... | collective-permute-start | bytes 1966088 | tf_op jit(solution)/shard_map/ppermute | solution.py:22
  33.4 2.4 copy-start.1
  35.8 25.7 %collective-permute-start.5 = (bf16[320,1024]{1,0:T(8,128)(2,1)S(1)}, bf16[320,1024]{1,0:T(8,128)(2,1)S(1)}, u32[]{:S(2)}, u32[]{:S(2)}) collective-permute-start(bf16[320,1024]{1,0:T(8,128)(2,1)S(1)} %collective-permute-done.3), channel_id=1, source_target_pairs={{0,96},{1,97},{2,98},{3,99},{4,100},{5,101},{6,102},{7,103},{8,104... | collective-permute-start | bytes 1966088 | tf_op jit(solution)/shard_map/ppermute | solution.py:22
  38.5 32.9 %collective-permute-start.6 = (bf16[320,1024]{1,0:T(8,128)(2,1)S(1)}, bf16[320,1024]{1,0:T(8,128)(2,1)S(1)}, u32[]{:S(2)}, u32[]{:S(2)}) collective-permute-start(bf16[320,1024]{1,0:T(8,128)(2,1)S(1)} %collective-permute-done.3), channel_id=1, source_target_pairs={{0,64},{1,65},{2,66},{3,67},{4,68},{5,69},{6,70},{7,71},{8,72},{9,... | collective-permute-start | bytes 1966088 | tf_op jit(solution)/shard_map/ppermute | solution.py:22
  82.5 2.5 copy-start.2
  116.7 148.0 %copy-start.4 = (bf16[128,128]{1,0:T(8,128)(2,1)S(1)}, bf16[128,128]{1,0:T(8,128)(2,1)}, u32[]{:S(2)}) copy-start(bf16[128,128]{1,0:T(8,128)(2,1)} %param.17) | copy-start | bytes 98308
  116.7 26.4 %collective-permute-start.7 = (bf16[4,128,1024]{2,1,0:T(8,128)(2,1)S(1)}, bf16[4,128,1024]{2,1,0:T(8,128)(2,1)S(1)}, u32[]{:S(2)}, u32[]{:S(2)}) collective-permute-start(bf16[4,128,1024]{2,1,0:T(8,128)(2,1)S(1)} %get-tuple-element.7), channel_id=1, source_target_pairs={{0,32},{1,33},{2,34},{3,35},{4,36},{5,37},{6,38},{7,39},{8,40},{9,... | collective-permute-start | bytes 3145736 | tf_op jit(solution)/shard_map/ppermute | solution.py:22
  116.8 26.4 %collective-permute-start.8 = (bf16[4,128,1024]{2,1,0:T(8,128)(2,1)S(1)}, bf16[4,128,1024]{2,1,0:T(8,128)(2,1)S(1)}, u32[]{:S(2)}, u32[]{:S(2)}) collective-permute-start(bf16[4,128,1024]{2,1,0:T(8,128)(2,1)S(1)} %get-tuple-element.8), channel_id=1, source_target_pairs={{0,96},{1,97},{2,98},{3,99},{4,100},{5,101},{6,102},{7,103},{8,104... | collective-permute-start | bytes 3145736 | tf_op jit(solution)/shard_map/ppermute | solution.py:22
  119.5 44.8 %collective-permute-start.9 = (bf16[4,128,1024]{2,1,0:T(8,128)(2,1)S(1)}, bf16[4,128,1024]{2,1,0:T(8,128)(2,1)S(1)}, u32[]{:S(2)}, u32[]{:S(2)}) collective-permute-start(bf16[4,128,1024]{2,1,0:T(8,128)(2,1)S(1)} %get-tuple-element.9), channel_id=1, source_target_pairs={{0,64},{1,65},{2,66},{3,67},{4,68},{5,69},{6,70},{7,71},{8,72},{9,... | collective-permute-start | bytes 3145736 | tf_op jit(solution)/shard_map/ppermute | solution.py:22
  166.1 19.1 %collective-permute-start.10 = (bf16[128,1024]{1,0:T(8,128)(2,1)}, bf16[128,1024]{1,0:T(8,128)(2,1)S(1)}, u32[]{:S(2)}, u32[]{:S(2)}) collective-permute-start(bf16[128,1024]{1,0:T(8,128)(2,1)} %get-tuple-element.14), channel_id=1, source_target_pairs={{0,0},{1,1},{2,16},{3,17},{4,32},{5,33},{6,48},{7,49},{8,64},{9,65... | collective-permute-start | bytes 786440 | tf_op jit(solution)/shard_map/ppermute | solution.py:22
  172.5 36.2 %collective-permute-start.11 = (bf16[128,1024]{1,0:T(8,128)(2,1)}, bf16[128,1024]{1,0:T(8,128)(2,1)S(1)}, u32[]{:S(2)}, u32[]{:S(2)}) collective-permute-start(bf16[128,1024]{1,0:T(8,128)(2,1)} %get-tuple-element.17), channel_id=1, source_target_pairs={{0,1},{1,0},{2,17},{3,16},{4,33},{5,32},{6,49},{7,48},{8,65},{9,64... | collective-permute-start | bytes 786440 | tf_op jit(solution)/shard_map/ppermute | solution.py:22
  176.0 79.1 %collective-permute-start.12 = (bf16[128,1024]{1,0:T(8,128)(2,1)}, bf16[128,1024]{1,0:T(8,128)(2,1)S(1)}, u32[]{:S(2)}, u32[]{:S(2)}) collective-permute-start(bf16[128,1024]{1,0:T(8,128)(2,1)} %get-tuple-element.16), channel_id=1, source_target_pairs={{0,2},{1,3},{2,18},{3,19},{4,34},{5,35},{6,50},{7,51},{8,66},{9,67... | collective-permute-start | bytes 786440 | tf_op jit(solution)/shard_map/ppermute | solution.py:22
  176.5 87.9 %collective-permute-start.13 = (bf16[128,1024]{1,0:T(8,128)(2,1)S(1)}, bf16[128,1024]{1,0:T(8,128)(2,1)S(1)}, u32[]{:S(2)}, u32[]{:S(2)}) collective-permute-start(bf16[128,1024]{1,0:T(8,128)(2,1)S(1)} %get-tuple-element.15), channel_id=1, source_target_pairs={{0,3},{1,2},{2,19},{3,18},{4,35},{5,34},{6,51},{7,50},{8,67},{9,66... | collective-permute-start | bytes 786440 | tf_op jit(solution)/shard_map/ppermute | solution.py:22
Sparse Core Ops, SparseCore 0:
  11.0 71.4 all-gather.1

commit v2 on v0

v2 whole, which is shorter than its diff:
```python
import math

import jax
import jax.numpy as jnp
from jax import lax
from jax.sharding import PartitionSpec as P

N_ROW = 8
N_COL = 16
BOTH = ("row", "col")
PARTS = 2

SLAB_PAIR = (
    (0, 7, 3, 5, 4, 6, 1, 2),
    (2, 5, 1, 7, 0, 4, 3, 6),
    (7, 3, 4, 2, 6, 0, 5, 1),
    (0, 1, 5, 3, 7, 2, 6, 4),
    (6, 4, 2, 0, 1, 3, 5, 7),
    (3, 1, 4, 6, 2, 0, 7, 5),
    (4, 0, 7, 6, 5, 3, 2, 1),
    (5, 6, 2, 0, 4, 1, 7, 3),
    (7, 0, 4, 5, 6, 2, 3, 1),
    (5, 2, 6, 3, 7, 1, 0, 4),
    (1, 4, 3, 6, 2, 7, 0, 5),
    (7, 2, 5, 0, 4, 1, 3, 6),
    (6, 4, 7, 2, 1, 0, 5, 3),
    (0, 3, 2, 1, 7, 5, 6, 4),
    (0, 3, 1, 6, 5, 4, 2, 7),
    (2, 5, 0, 4, 3, 7, 1, 6),
)


def send(x, to):
    pairs = []
    for r in range(N_ROW):
        for c in range(N_COL):
            rr, cc = to(r, c)
            pairs.append((r * N_COL + c, rr * N_COL + cc))
    return lax.ppermute(x, BOTH, pairs)


def along_y(step):
    return lambda r, c: ((r + 2 * step) % N_ROW, c)


def flip_x(r, c):
    return r ^ 1, c


def owner_of(j):
    return lambda r, c: (c // 2, 2 * SLAB_PAIR[c][r] + (j ^ (c % 2)))


def add(*terms):
    total = terms[0].astype(jnp.float32)
    for term in terms[1:]:
        total = total + term.astype(jnp.float32)
    return total.astype(jnp.bfloat16)


def shards(
    coef_occ,
    coef_resp,
    orb_energy,
    lap_index,
    density_mask,
    tri_blocks,
    block_ao,
    block_slab,
    metric,
):
    row, col = lax.axis_index("row"), lax.axis_index("col")
    y, x, core = row // 2, row % 2, col % 2
    t_point = 0.04 * jnp.exp(0.5 * math.log(2.0) * lap_index[0].astype(jnp.float32))
    weighted = (coef_occ.astype(jnp.float32) * jnp.exp(t_point * orb_energy)[None, :]).astype(
        jnp.bfloat16
    )
    w_all = lax.all_gather(weighted.T, "col", axis=0, tiled=True)

    mine = coef_resp.T
    other = send(mine, flip_x)
    depth, cols_here = mine.shape
    width = cols_here // PARTS
    r_all = [jnp.zeros((N_ROW * depth, width), mine.dtype) for _ in range(PARTS)]

    def place(r_all, part, step, xx):
        at = (((y + 4 - step) % 4) * 2 + xx) * depth
        return [
            lax.dynamic_update_slice(whole, part[:, h * width : (h + 1) * width], (at, 0))
            for h, whole in enumerate(r_all)
        ]

    r_all = place(r_all, mine, 0, x)
    for step in (1, 3, 2):
        r_all = place(r_all, send(mine, along_y(step)), step, x)
    r_all = place(r_all, other, 0, 1 - x)
    for step in (1, 3, 2):
        r_all = place(r_all, send(other, along_y(step)), step, 1 - x)

    table = lax.dynamic_slice(jnp.asarray(SLAB_PAIR, jnp.int32), (col, 0), (1, N_ROW))[0]
    here = jnp.arange(N_COL, dtype=jnp.int32)
    pair_at = jnp.sum(
        jnp.where(
            jnp.arange(N_ROW, dtype=jnp.int32)[None, :]
            == (((y + here // 4) % 4) * 2 + (x + here // 2 % 2) % 2)[:, None],
            table[None, :],
            0,
        ),
        axis=1,
    )
    slab_at = 2 * pair_at + ((here % 2) ^ core)
    n_ao = coef_occ.shape[0] // 128
    chosen = (block_slab[0][None, None, :] == slab_at[:, None, None]) & (
        block_ao[0][None, None, :] == jnp.arange(n_ao, dtype=jnp.int32)[None, :, None]
    )
    blocks = jnp.einsum(
        "sab,bqm->saqm",
        chosen.astype(jnp.bfloat16),
        tri_blocks[0].transpose(0, 2, 1),
        preferred_element_type=jnp.float32,
    ).astype(jnp.bfloat16)
    matrix = blocks.transpose(0, 2, 1, 3).reshape(N_COL * 128, n_ao * 128)

    rows_here = coef_occ.shape[0]
    mask = density_mask.astype(jnp.float32)
    mask_cols = mask.shape[1] // PARTS
    pseudo, grads = [], []
    for h in range(PARTS):
        r_part = r_all[h]
        if h:
            r_part, low_far, high_far = lax.optimization_barrier((r_part, low_far, high_far))
        product = lax.dot_general(
            w_all, r_part, (((0,), (0,)), ((), ())), preferred_element_type=jnp.float32
        )
        masked = (
            product.reshape(n_ao, 128, mask_cols, 128)
            * mask[:, None, h * mask_cols : (h + 1) * mask_cols, None]
        )
        part = masked.reshape(rows_here, width).astype(jnp.bfloat16)
        pseudo.append(part)

        piece = [None] * 8
        for n in (4, 5, 3, 6, 2, 7, 1, 0):
            piece[n] = jnp.dot(
                matrix[n * 256 : (n + 1) * 256], part, preferred_element_type=jnp.float32
            ).astype(jnp.bfloat16)
        low_far = send(piece[4], along_y(1))
        high_far = send(piece[5], along_y(-1))
        high_up = send(piece[3], along_y(1))
        low_down = send(piece[6], along_y(-1))
        high_down = send(add(piece[7], high_far), along_y(-1))
        low_up = send(add(piece[2], low_far), along_y(1))
        crossed = send(add(piece[1], high_up, high_down), flip_x)
        total = [
            add(piece[0][128 * j : 128 * j + 128], low_down[128 * j : 128 * j + 128],
                low_up[128 * j : 128 * j + 128], crossed[128 * j : 128 * j + 128])
            for j in range(2)
        ]
        got = [send(total[j], owner_of(j)) for j in range(2)]
        grads.append(
            [
                lax.dot_general(
                    jnp.where(core == 0, got[e], got[1 - e]),
                    metric,
                    (((0,), (1,)), ((), ())),
                    preferred_element_type=jnp.float32,
                ).astype(jnp.bfloat16)
                for e in range(2)
            ]
        )
    pseudo, low_far = lax.optimization_barrier((pseudo, low_far))
    grad = jnp.concatenate([grads[h][e] for e in range(2) for h in range(PARTS)], axis=0)
    return (jnp.concatenate(pseudo, axis=1), grad)


def solution(mesh):
    placed = (
        P("row", "col"),
        P("col", "row"),
        P("col"),
        P(),
        P("row", "col"),
        P("row", None, None, None),
        P("row", None),
        P("row", None),
        P("col", None),
    )
    return jax.shard_map(
        shards,
        mesh=mesh,
        in_specs=placed,
        out_specs=(P("row", "col"), P("row", "col")),
        check_vma=False,
    )
```

time: 505 us -> 190 us (0.38)
  the two profiles are of different devices: /device:TPU:103 before, /device:TPU:29 now
where the time goes in v2:
time: 190 us
  waiting for transfers between devices  75.2 us (40%)
  starting transfers between devices  41.2 us (22%)
  matrix products  29.7 us (16%)
  local copies, waits for them, and re-layouts  21 us (11%)
  between operations  15.2 us (8%)
  other arithmetic  7.65 us (4%)
    ppermute x25, waiting for transfers between devices, send(): return lax.ppermute(x, BOTH, pairs)  58.8 us
    ppermute x25, starting transfers between devices, send(): return lax.ppermute(x, BOTH, pairs)  41.2 us
    all_gather x1, waiting for transfers between devices, shards(): w_all = lax.all_gather(weighted.T, 'col', axis=0, tiled=True)  16.3 us
    dot_general x2, matrix products, shards(): lax.dot_general(w_all, r_part, (((0,), (0,)), ((), ())), preferred_elemen...  15.1 us
    dot_general x16, matrix products, shards(): jnp.dot(matrix[n * 256:(n + 1) * 256], part, preferred_element_type=jnp.f...  11.5 us
    dynamic_update_slice x9, local copies, waits for them, and re-layouts, place(): lax.dynamic_update_slice(whole, part[:, h * width:(h + 1) * width], (at, 0))  9.4 us
  transfers between devices with their start and end apart: 26, of which 11 were waited for; matrix products, arithmetic and copies ran while one was open for 22% of the time, Pallas kernels for 0%

profile of v2, /device:TPU:29, one launch (start us, length us, event | category | flops | bytes accessed | tf_op | source)
XLA Modules:
  0.0 189.9 jit_solution(391524098743538436)
XLA Ops:
  8.6 2.1 %fusion.41 = bf16[160,2048]{1,0:T(8,128)(2,1)} fusion(bf16[2048,160]{0,1:T(8,128)(2,1)} %param.10, f32[160]{0:T(256)S(1)} %multiply_exponential_fusion), kind=kLoop, calls=%fused_computation.66 | loop fusion | flops 983040 | bytes 1311360 | tf_op jit(solution)/shard_map/transpose | solution.py:78
  14.1 3.3 %copy.16 = bf16[64,128,128]{2,0,1:T(8,128)(2,1)S(1)} copy(bf16[64,128,128]{1,2,0:T(8,128)(2,1)} %bitcast.123) | data formatting | bytes 4194304 | tf_op jit(solution)/shard_map/transpose | solution.py:119
  18.3 2.3 %convert_bitcast_fusion = bf16[16,128,16,128]{3,2,1,0:T(8,128)(2,1)S(1)} fusion(bf16[64,128,128]{2,0,1:T(8,128)(2,1)S(1)} %copy.16, pred[16,64]{1,0:T(8,128)(4,1)S(1)} %get-tuple-element.36, pred[16,64]{1,0:T(8,128)(4,1)S(1)} %get-tuple-element.37), kind=kOutput, calls=%fused_computation | convolution fusion | flops 541081600 | bytes 10487808 | tf_op jit(solution)/shard_map/sab,bqm->saqm/dot_general | solution.py:116
  20.7 3.4 %fusion.64 = (bf16[2,128,16,128]{3,2,1,0:T(8,128)(2,1)}, bf16[2,128,16,128]{3,2,1,0:T(8,128)(2,1)}, bf16[2,128,16,128]{3,2,1,0:T(8,128)(2,1)}, bf16[2,128,16,128...) fusion(bf16[16,128,16,128]{3,2,1,0:T(8,128)(2,1)S(1)} %convert_, ...), kind=kLoop, calls=%fused_computation.139 | loop fusion | bytes 16777216 | tf_op jit(solution)/shard_map/slice | solution.py:145
  26.9 9.0 %collective-permute-done.3 = bf16[320,1024]{1,0:T(8,128)(2,1)S(1)} collective-permute-done((bf16[320,1024]{1,0:T(8,128)(2,1)}, bf16[320,1024]{1,0:T(8,128)(2,1)S(1)}, u32[]{:S(2)}, u32[]{:S(2)}) %collective-permute-start.3) | collective-permute-done | bytes 655392 | tf_op jit(solution)/shard_map/ppermute | solution.py:39
  35.9 3.8 %collective-permute-start.4 = (bf16[320,1024]{1,0:T(8,128)(2,1)S(1)}, bf16[320,1024]{1,0:T(8,128)(2,1)S(1)}, u32[]{:S(2)}, u32[]{:S(2)}) collective-permute-start(bf16[320,1024]{1,0:T(8,128)(2,1)S(1)} %collective-permute-done.3), channel_id=1, source_target_pairs={{0,32},{1,33},{2,34},{3,35},{4,36},{5,37},{6,38},{7,39},{8,40},{9,... | collective-permute-start | bytes 1966088 | tf_op jit(solution)/shard_map/ppermute | solution.py:39
  42.8 1.9 slice_dynamic-update-slice_fusion.5
  47.3 4.9 %collective-permute-done.4 = bf16[320,1024]{1,0:T(8,128)(2,1)S(1)} collective-permute-done((bf16[320,1024]{1,0:T(8,128)(2,1)S(1)}, bf16[320,1024]{1,0:T(8,128)(2,1)S(1)}, u32[]{:S(2)}, u32[]{:S(2)}) %collective-permute-start.4) | collective-permute-done | bytes 655392 | tf_op jit(solution)/shard_map/ppermute | solution.py:39
  53.7 10.9 %collective-permute-done.6 = bf16[320,1024]{1,0:T(8,128)(2,1)S(1)} collective-permute-done((bf16[320,1024]{1,0:T(8,128)(2,1)S(1)}, bf16[320,1024]{1,0:T(8,128)(2,1)S(1)}, u32[]{:S(2)}, u32[]{:S(2)}) %collective-permute-start.6) | collective-permute-done | bytes 655392 | tf_op jit(solution)/shard_map/ppermute | solution.py:39
  65.4 16.3 %all-gather.2.cloned.1.call-done = bf16[2560,2048]{1,0:T(8,128)(2,1)} async-done(((bf16[160,2048]{1,0:T(8,128)(2,1)}), bf16[2560,2048]{1,0:T(8,128)(2,1)}) %all-gather.2.cloned.1.call-update) | async-done | bytes 10485776 | tf_op jit(solution)/shard_map/all_gather | solution.py:78
  82.3 9.2 %fusion.1 = bf16[2048,512]{1,0:T(8,128)(2,1)S(1)} fusion(f32[256,8,4,128]{3,2,1,0:T(4,128)S(1)} %bitcast.122, bf16[2560,2048]{1,0:T(8,128)(2,1)} %all-gather.2.cloned.1.call-done, bf16[2560,512]{1,0:T(8,128)(2,1)} %get-tuple-element.21), kind=kOutput, calls=%fused_computation.4 | convolution fusion | flops 5370806272 | bytes 19398656 | tf_op jit(solution)/shard_map/dot_general | solution.py:132
  92.3 2.0 %collective-permute-start.7 = (bf16[256,512]{1,0:T(8,128)(2,1)S(1)}, bf16[256,512]{1,0:T(8,128)(2,1)S(1)}, u32[]{:S(2)}, u32[]{:S(2)}) collective-permute-start(bf16[256,512]{1,0:T(8,128)(2,1)S(1)} %convolution_convert_fusion.15), channel_id=1, source_target_pairs={{0,32},{1,33},{2,34},{3,35},{4,36},{5,37},{6,38},{7,39},{8,40},{9,... | collective-permute-start | bytes 786440 | tf_op jit(solution)/shard_map/ppermute | solution.py:39
  96.0 2.7 %collective-permute-start.12 = (bf16[256,512]{1,0:T(8,128)(2,1)S(1)}, bf16[256,512]{1,0:T(8,128)(2,1)S(1)}, u32[]{:S(2)}, u32[]{:S(2)}) collective-permute-start(bf16[256,512]{1,0:T(8,128)(2,1)S(1)} %convolution_convert_fusion.8), channel_id=1, source_target_pairs={{0,32},{1,33},{2,34},{3,35},{4,36},{5,37},{6,38},{7,39},{8,40},{9,... | collective-permute-start | bytes 786440 | tf_op jit(solution)/shard_map/ppermute | solution.py:39
  101.4 2.3 %collective-permute-done.8 = bf16[256,512]{1,0:T(8,128)(2,1)S(1)} collective-permute-done((bf16[256,512]{1,0:T(8,128)(2,1)S(1)}, bf16[256,512]{1,0:T(8,128)(2,1)S(1)}, u32[]{:S(2)}, u32[]{:S(2)}) %collective-permute-start.8) | collective-permute-done | bytes 262176 | tf_op jit(solution)/shard_map/ppermute | solution.py:39
  104.4 5.8 %fusion = bf16[2048,512]{1,0:T(8,128)(2,1)S(1)} fusion(f32[256,8,4,128]{3,2,1,0:T(4,128)S(1)} %bitcast.121, bf16[2560,2048]{1,0:T(8,128)(2,1)S(1)} %copy-done.13, bf16[2560,512]{1,0:T(8,128)(2,1)S(1)} %get-tuple-element.5), kind=kOutput, calls=%fused_computation.2 | convolution fusion | flops 5370806272 | bytes 19398656 | tf_op jit(solution)/shard_map/dot_general | solution.py:132
  116.7 2.7 %collective-permute-start.11 = (bf16[256,512]{1,0:T(8,128)(2,1)S(1)}, bf16[256,512]{1,0:T(8,128)(2,1)S(1)}, u32[]{:S(2)}, u32[]{:S(2)}) collective-permute-start(bf16[256,512]{1,0:T(8,128)(2,1)S(1)} %add_convert_fusion.5), channel_id=1, source_target_pairs={{0,32},{1,33},{2,34},{3,35},{4,36},{5,37},{6,38},{7,39},{8,40},{9,... | collective-permute-start | bytes 786440 | tf_op jit(solution)/shard_map/ppermute | solution.py:39
  122.4 5.5 %collective-permute-done.20 = bf16[256,512]{1,0:T(8,128)(2,1)S(1)} collective-permute-done((bf16[256,512]{1,0:T(8,128)(2,1)S(1)}, bf16[256,512]{1,0:T(8,128)(2,1)S(1)}, u32[]{:S(2)}, u32[]{:S(2)}) %collective-permute-start.20) | collective-permute-done | bytes 262176 | tf_op jit(solution)/shard_map/ppermute | solution.py:39
  134.7 3.5 %collective-permute-start.15 = (bf16[128,512]{1,0:T(8,128)(2,1)S(1)}, bf16[128,512]{1,0:T(8,128)(2,1)S(1)}, u32[]{:S(2)}, u32[]{:S(2)}) collective-permute-start(bf16[128,512]{1,0:T(8,128)(2,1)S(1)} %get-tuple-element.16), channel_id=1, source_target_pairs={{0,0},{1,5},{2,30},{3,17},{4,44},{5,39},{6,56},{7,59},{8,78},{9,75... | collective-permute-start | bytes 393224 | tf_op jit(solution)/shard_map/ppermute | solution.py:39
  138.2 8.8 %collective-permute-start.16 = (bf16[128,512]{1,0:T(8,128)(2,1)S(1)}, bf16[128,512]{1,0:T(8,128)(2,1)S(1)}, u32[]{:S(2)}, u32[]{:S(2)}) collective-permute-start(bf16[128,512]{1,0:T(8,128)(2,1)S(1)} %get-tuple-element.17), channel_id=1, source_target_pairs={{0,1},{1,4},{2,31},{3,16},{4,45},{5,38},{6,57},{7,58},{8,79},{9,74... | collective-permute-start | bytes 393224 | tf_op jit(solution)/shard_map/ppermute | solution.py:39
  148.2 2.7 %pad_maximum_fusion = bf16[2048,1024]{1,0:T(8,128)(2,1)} fusion(bf16[2048,512]{1,0:T(8,128)(2,1)S(1)} %fusion, bf16[2048,512]{1,0:T(8,128)(2,1)S(1)} %fusion.1), kind=kLoop, calls=%fused_computation.5 | loop fusion | flops 8388608 | bytes 8388608 | tf_op jit(solution)/shard_map/concatenate | solution.py:173
  150.9 8.5 %collective-permute-done.16 = bf16[128,512]{1,0:T(8,128)(2,1)S(1)} collective-permute-done((bf16[128,512]{1,0:T(8,128)(2,1)S(1)}, bf16[128,512]{1,0:T(8,128)(2,1)S(1)}, u32[]{:S(2)}, u32[]{:S(2)}) %collective-permute-start.16) | collective-permute-done | bytes 131104 | tf_op jit(solution)/shard_map/ppermute | solution.py:39
  159.8 6.3 %collective-permute-start.23 = (bf16[128,512]{1,0:T(8,128)(2,1)S(1)}, bf16[128,512]{1,0:T(8,128)(2,1)S(1)}, u32[]{:S(2)}, u32[]{:S(2)}) collective-permute-start(bf16[128,512]{1,0:T(8,128)(2,1)S(1)} %get-tuple-element.18), channel_id=1, source_target_pairs={{0,0},{1,5},{2,30},{3,17},{4,44},{5,39},{6,56},{7,59},{8,78},{9,75... | collective-permute-start | bytes 393224 | tf_op jit(solution)/shard_map/ppermute | solution.py:39
  166.7 8.7 %collective-permute-done.23 = bf16[128,512]{1,0:T(8,128)(2,1)S(1)} collective-permute-done((bf16[128,512]{1,0:T(8,128)(2,1)S(1)}, bf16[128,512]{1,0:T(8,128)(2,1)S(1)}, u32[]{:S(2)}, u32[]{:S(2)}) %collective-permute-start.23) | collective-permute-done | bytes 131104 | tf_op jit(solution)/shard_map/ppermute | solution.py:39
  175.4 6.4 %collective-permute-done.24 = bf16[128,512]{1,0:T(8,128)(2,1)S(1)} collective-permute-done((bf16[128,512]{1,0:T(8,128)(2,1)S(1)}, bf16[128,512]{1,0:T(8,128)(2,1)S(1)}, u32[]{:S(2)}, u32[]{:S(2)}) %collective-permute-start.24) | collective-permute-done | bytes 131104 | tf_op jit(solution)/shard_map/ppermute | solution.py:39
  (112 shorter events, 41.5 us)
Async XLA Ops:
  7.2 74.5 %all-gather.2.cloned.1.call-start = ((), (), s32[]{:S(2)}) async-start(), calls=%async_computation | async-start | bytes 11141120 | tf_op jit(solution)/shard_map/all_gather | solution.py:78
  10.7 29.0 %collective-permute-start = (bf16[320,1024]{1,0:T(8,128)(2,1)}, bf16[320,1024]{1,0:T(8,128)(2,1)}, u32[]{:S(2)}, u32[]{:S(2)}) collective-permute-start(bf16[320,1024]{1,0:T(8,128)(2,1)} %bitcast.140), channel_id=1, source_target_pairs={{0,32},{1,33},{2,34},{3,35},{4,36},{5,37},{6,38},{7,39},{8,40},{9,... | collective-permute-start | bytes 1966088 | tf_op jit(solution)/shard_map/ppermute | solution.py:39
  10.8 32.0 %collective-permute-start.1 = (bf16[320,1024]{1,0:T(8,128)(2,1)}, bf16[320,1024]{1,0:T(8,128)(2,1)}, u32[]{:S(2)}, u32[]{:S(2)}) collective-permute-start(bf16[320,1024]{1,0:T(8,128)(2,1)} %bitcast.141), channel_id=1, source_target_pairs={{0,96},{1,97},{2,98},{3,99},{4,100},{5,101},{6,102},{7,103},{8,104... | collective-permute-start | bytes 1966088 | tf_op jit(solution)/shard_map/ppermute | solution.py:39
  12.3 32.4 %collective-permute-start.2 = (bf16[320,1024]{1,0:T(8,128)(2,1)}, bf16[320,1024]{1,0:T(8,128)(2,1)}, u32[]{:S(2)}, u32[]{:S(2)}) collective-permute-start(bf16[320,1024]{1,0:T(8,128)(2,1)} %bitcast.142), channel_id=1, source_target_pairs={{0,64},{1,65},{2,66},{3,67},{4,68},{5,69},{6,70},{7,71},{8,72},{9,... | collective-permute-start | bytes 1966088 | tf_op jit(solution)/shard_map/ppermute | solution.py:39
  13.2 22.7 %collective-permute-start.3 = (bf16[320,1024]{1,0:T(8,128)(2,1)}, bf16[320,1024]{1,0:T(8,128)(2,1)S(1)}, u32[]{:S(2)}, u32[]{:S(2)}) collective-permute-start(bf16[320,1024]{1,0:T(8,128)(2,1)} %bitcast.143), channel_id=1, source_target_pairs={{0,16},{1,17},{2,18},{3,19},{4,20},{5,21},{6,22},{7,23},{8,24},{9,... | collective-permute-start | bytes 1966088 | tf_op jit(solution)/shard_map/ppermute | solution.py:39
  35.9 16.3 %collective-permute-start.4 = (bf16[320,1024]{1,0:T(8,128)(2,1)S(1)}, bf16[320,1024]{1,0:T(8,128)(2,1)S(1)}, u32[]{:S(2)}, u32[]{:S(2)}) collective-permute-start(bf16[320,1024]{1,0:T(8,128)(2,1)S(1)} %collective-permute-done.3), channel_id=1, source_target_pairs={{0,32},{1,33},{2,34},{3,35},{4,36},{5,37},{6,38},{7,39},{8,40},{9,... | collective-permute-start | bytes 1966088 | tf_op jit(solution)/shard_map/ppermute | solution.py:39
  39.7 13.2 %collective-permute-start.5 = (bf16[320,1024]{1,0:T(8,128)(2,1)S(1)}, bf16[320,1024]{1,0:T(8,128)(2,1)S(1)}, u32[]{:S(2)}, u32[]{:S(2)}) collective-permute-start(bf16[320,1024]{1,0:T(8,128)(2,1)S(1)} %collective-permute-done.3), channel_id=1, source_target_pairs={{0,96},{1,97},{2,98},{3,99},{4,100},{5,101},{6,102},{7,103},{8,104... | collective-permute-start | bytes 1966088 | tf_op jit(solution)/shard_map/ppermute | solution.py:39
  39.7 24.9 %collective-permute-start.6 = (bf16[320,1024]{1,0:T(8,128)(2,1)S(1)}, bf16[320,1024]{1,0:T(8,128)(2,1)S(1)}, u32[]{:S(2)}, u32[]{:S(2)}) collective-permute-start(bf16[320,1024]{1,0:T(8,128)(2,1)S(1)} %collective-permute-done.3), channel_id=1, source_target_pairs={{0,64},{1,65},{2,66},{3,67},{4,68},{5,69},{6,70},{7,71},{8,72},{9,... | collective-permute-start | bytes 1966088 | tf_op jit(solution)/shard_map/ppermute | solution.py:39
  92.3 9.1 %collective-permute-start.7 = (bf16[256,512]{1,0:T(8,128)(2,1)S(1)}, bf16[256,512]{1,0:T(8,128)(2,1)S(1)}, u32[]{:S(2)}, u32[]{:S(2)}) collective-permute-start(bf16[256,512]{1,0:T(8,128)(2,1)S(1)} %convolution_convert_fusion.15), channel_id=1, source_target_pairs={{0,32},{1,33},{2,34},{3,35},{4,36},{5,37},{6,38},{7,39},{8,40},{9,... | collective-permute-start | bytes 786440 | tf_op jit(solution)/shard_map/ppermute | solution.py:39
  95.0 8.8 %collective-permute-start.8 = (bf16[256,512]{1,0:T(8,128)(2,1)S(1)}, bf16[256,512]{1,0:T(8,128)(2,1)S(1)}, u32[]{:S(2)}, u32[]{:S(2)}) collective-permute-start(bf16[256,512]{1,0:T(8,128)(2,1)S(1)} %convolution_convert_fusion.14), channel_id=1, source_target_pairs={{0,96},{1,97},{2,98},{3,99},{4,100},{5,101},{6,102},{7,103},{8,104... | collective-permute-start | bytes 786440 | tf_op jit(solution)/shard_map/ppermute | solution.py:39
  96.0 23.4 %collective-permute-start.12 = (bf16[256,512]{1,0:T(8,128)(2,1)S(1)}, bf16[256,512]{1,0:T(8,128)(2,1)S(1)}, u32[]{:S(2)}, u32[]{:S(2)}) collective-permute-start(bf16[256,512]{1,0:T(8,128)(2,1)S(1)} %convolution_convert_fusion.8), channel_id=1, source_target_pairs={{0,32},{1,33},{2,34},{3,35},{4,36},{5,37},{6,38},{7,39},{8,40},{9,... | collective-permute-start | bytes 786440 | tf_op jit(solution)/shard_map/ppermute | solution.py:39
  100.2 30.5 %collective-permute-start.10 = (bf16[256,512]{1,0:T(8,128)(2,1)S(1)}, bf16[256,512]{1,0:T(8,128)(2,1)S(1)}, u32[]{:S(2)}, u32[]{:S(2)}) collective-permute-start(bf16[256,512]{1,0:T(8,128)(2,1)S(1)} %convolution_convert_fusion.11), channel_id=1, source_target_pairs={{0,96},{1,97},{2,98},{3,99},{4,100},{5,101},{6,102},{7,103},{8,104... | collective-permute-start | bytes 786440 | tf_op jit(solution)/shard_map/ppermute | solution.py:39
  115.2 12.7 %collective-permute-start.20 = (bf16[256,512]{1,0:T(8,128)(2,1)S(1)}, bf16[256,512]{1,0:T(8,128)(2,1)S(1)}, u32[]{:S(2)}, u32[]{:S(2)}) collective-permute-start(bf16[256,512]{1,0:T(8,128)(2,1)S(1)} %convolution_convert_fusion), channel_id=1, source_target_pairs={{0,96},{1,97},{2,98},{3,99},{4,100},{5,101},{6,102},{7,103},{8,104... | collective-permute-start | bytes 786440 | tf_op jit(solution)/shard_map/ppermute | solution.py:39
  116.7 15.2 %collective-permute-start.11 = (bf16[256,512]{1,0:T(8,128)(2,1)S(1)}, bf16[256,512]{1,0:T(8,128)(2,1)S(1)}, u32[]{:S(2)}, u32[]{:S(2)}) collective-permute-start(bf16[256,512]{1,0:T(8,128)(2,1)S(1)} %add_convert_fusion.5), channel_id=1, source_target_pairs={{0,32},{1,33},{2,34},{3,35},{4,36},{5,37},{6,38},{7,39},{8,40},{9,... | collective-permute-start | bytes 786440 | tf_op jit(solution)/shard_map/ppermute | solution.py:39
  119.5 10.4 %collective-permute-start.9 = (bf16[256,512]{1,0:T(8,128)(2,1)S(1)}, bf16[256,512]{1,0:T(8,128)(2,1)S(1)}, u32[]{:S(2)}, u32[]{:S(2)}) collective-permute-start(bf16[256,512]{1,0:T(8,128)(2,1)S(1)} %convolution_convert_fusion.13), channel_id=1, source_target_pairs={{0,32},{1,33},{2,34},{3,35},{4,36},{5,37},{6,38},{7,39},{8,40},{9,... | collective-permute-start | bytes 786440 | tf_op jit(solution)/shard_map/ppermute | solution.py:39
  122.3 16.0 %collective-permute-start.19 = (bf16[256,512]{1,0:T(8,128)(2,1)S(1)}, bf16[256,512]{1,0:T(8,128)(2,1)S(1)}, u32[]{:S(2)}, u32[]{:S(2)}) collective-permute-start(bf16[256,512]{1,0:T(8,128)(2,1)S(1)} %convolution_convert_fusion.2), channel_id=1, source_target_pairs={{0,32},{1,33},{2,34},{3,35},{4,36},{5,37},{6,38},{7,39},{8,40},{9,... | collective-permute-start | bytes 786440 | tf_op jit(solution)/shard_map/ppermute | solution.py:39
  129.8 17.3 %collective-permute-start.21 = (bf16[256,512]{1,0:T(8,128)(2,1)S(1)}, bf16[256,512]{1,0:T(8,128)(2,1)S(1)}, u32[]{:S(2)}, u32[]{:S(2)}) collective-permute-start(bf16[256,512]{1,0:T(8,128)(2,1)S(1)} %add_convert_fusion.1), channel_id=1, source_target_pairs={{0,96},{1,97},{2,98},{3,99},{4,100},{5,101},{6,102},{7,103},{8,104... | collective-permute-start | bytes 786440 | tf_op jit(solution)/shard_map/ppermute | solution.py:39
  130.7 28.9 %collective-permute-start.17 = (bf16[256,512]{1,0:T(8,128)(2,1)S(1)}, bf16[256,512]{1,0:T(8,128)(2,1)S(1)}, u32[]{:S(2)}, u32[]{:S(2)}) collective-permute-start(bf16[256,512]{1,0:T(8,128)(2,1)S(1)} %convolution_convert_fusion.5), channel_id=1, source_target_pairs={{0,96},{1,97},{2,98},{3,99},{4,100},{5,101},{6,102},{7,103},{8,104... | collective-permute-start | bytes 786440 | tf_op jit(solution)/shard_map/ppermute | solution.py:39
  132.0 27.7 %collective-permute-start.18 = (bf16[256,512]{1,0:T(8,128)(2,1)S(1)}, bf16[256,512]{1,0:T(8,128)(2,1)S(1)}, u32[]{:S(2)}, u32[]{:S(2)}) collective-permute-start(bf16[256,512]{1,0:T(8,128)(2,1)S(1)} %add_convert_fusion.2), channel_id=1, source_target_pairs={{0,32},{1,33},{2,34},{3,35},{4,36},{5,37},{6,38},{7,39},{8,40},{9,... | collective-permute-start | bytes 786440 | tf_op jit(solution)/shard_map/ppermute | solution.py:39
  134.7 16.2 %collective-permute-start.15 = (bf16[128,512]{1,0:T(8,128)(2,1)S(1)}, bf16[128,512]{1,0:T(8,128)(2,1)S(1)}, u32[]{:S(2)}, u32[]{:S(2)}) collective-permute-start(bf16[128,512]{1,0:T(8,128)(2,1)S(1)} %get-tuple-element.16), channel_id=1, source_target_pairs={{0,0},{1,5},{2,30},{3,17},{4,44},{5,39},{6,56},{7,59},{8,78},{9,75... | collective-permute-start | bytes 393224 | tf_op jit(solution)/shard_map/ppermute | solution.py:39
  138.2 21.1 %collective-permute-start.16 = (bf16[128,512]{1,0:T(8,128)(2,1)S(1)}, bf16[128,512]{1,0:T(8,128)(2,1)S(1)}, u32[]{:S(2)}, u32[]{:S(2)}) collective-permute-start(bf16[128,512]{1,0:T(8,128)(2,1)S(1)} %get-tuple-element.17), channel_id=1, source_target_pairs={{0,1},{1,4},{2,31},{3,16},{4,45},{5,38},{6,57},{7,58},{8,79},{9,74... | collective-permute-start | bytes 393224 | tf_op jit(solution)/shard_map/ppermute | solution.py:39
  147.2 12.4 %collective-permute-start.22 = (bf16[256,512]{1,0:T(8,128)(2,1)S(1)}, bf16[256,512]{1,0:T(8,128)(2,1)S(1)}, u32[]{:S(2)}, u32[]{:S(2)}) collective-permute-start(bf16[256,512]{1,0:T(8,128)(2,1)S(1)} %add_convert_fusion), channel_id=1, source_target_pairs={{0,16},{1,17},{2,18},{3,19},{4,20},{5,21},{6,22},{7,23},{8,24},{9,... | collective-permute-start | bytes 786440 | tf_op jit(solution)/shard_map/ppermute | solution.py:39
  159.8 15.6 %collective-permute-start.23 = (bf16[128,512]{1,0:T(8,128)(2,1)S(1)}, bf16[128,512]{1,0:T(8,128)(2,1)S(1)}, u32[]{:S(2)}, u32[]{:S(2)}) collective-permute-start(bf16[128,512]{1,0:T(8,128)(2,1)S(1)} %get-tuple-element.18), channel_id=1, source_target_pairs={{0,0},{1,5},{2,30},{3,17},{4,44},{5,39},{6,56},{7,59},{8,78},{9,75... | collective-permute-start | bytes 393224 | tf_op jit(solution)/shard_map/ppermute | solution.py:39
  166.1 15.7 %collective-permute-start.24 = (bf16[128,512]{1,0:T(8,128)(2,1)S(1)}, bf16[128,512]{1,0:T(8,128)(2,1)S(1)}, u32[]{:S(2)}, u32[]{:S(2)}) collective-permute-start(bf16[128,512]{1,0:T(8,128)(2,1)S(1)} %get-tuple-element.19), channel_id=1, source_target_pairs={{0,1},{1,4},{2,31},{3,16},{4,45},{5,38},{6,57},{7,58},{8,79},{9,74... | collective-permute-start | bytes 393224 | tf_op jit(solution)/shard_map/ppermute | solution.py:39
  (16 other events, 216.6 us)
Sparse Core Ops, SparseCore 0:
  10.9 70.8 all-gather.1

commit v3 on v2

v3 whole, which is shorter than its diff:
```python
import math

import jax
import jax.numpy as jnp
from jax import lax
from jax.experimental import pallas as pl
from jax.experimental.pallas import tpu as pltpu
from jax.sharding import PartitionSpec as P

N_ROW = 8
N_COL = 16
BOTH = ("row", "col")
ORDER = (5, 3, 4, 7, 6, 2, 1, 0)

SLAB_PAIR = (
    (3, 5, 1, 4, 0, 7, 2, 6),
    (3, 6, 2, 7, 0, 5, 1, 4),
    (1, 4, 3, 6, 0, 2, 7, 5),
    (5, 0, 7, 2, 4, 6, 3, 1),
    (2, 1, 3, 0, 4, 5, 7, 6),
    (5, 4, 7, 6, 2, 3, 1, 0),
    (0, 3, 4, 6, 5, 2, 7, 1),
    (4, 3, 7, 1, 2, 0, 5, 6),
    (4, 2, 5, 0, 6, 3, 7, 1),
    (5, 0, 4, 2, 6, 3, 7, 1),
    (4, 7, 5, 6, 2, 1, 0, 3),
    (1, 0, 3, 2, 5, 7, 4, 6),
    (3, 4, 5, 1, 2, 0, 7, 6),
    (1, 2, 6, 7, 3, 5, 4, 0),
    (4, 5, 2, 0, 1, 7, 3, 6),
    (3, 6, 1, 5, 4, 7, 2, 0),
)


def send(x, to):
    pairs = []
    for r in range(N_ROW):
        for c in range(N_COL):
            rr, cc = to(r, c)
            pairs.append((r * N_COL + c, rr * N_COL + cc))
    return lax.ppermute(x, BOTH, pairs)


def along_y(step):
    return lambda r, c: ((r + 2 * step) % N_ROW, c)


def flip_x(r, c):
    return r ^ 1, c


def owner_of(j):
    return lambda r, c: (c // 2, 2 * SLAB_PAIR[c][r] + (j ^ (c % 2)))


def add(*terms):
    total = terms[0].astype(jnp.float32)
    for term in terms[1:]:
        total = total + term.astype(jnp.float32)
    return total.astype(jnp.bfloat16)


def pieces_kernel(matrix_ref, part_ref, *outs):
    value = jnp.dot(matrix_ref[...], part_ref[...], preferred_element_type=jnp.float32)
    for n, out in enumerate(outs):

        @pl.when(pl.program_id(0) == n)
        def _(out=out):
            out[...] = value.astype(out.dtype)


def pieces_of(matrix, part, first, count):
    depth, width = part.shape
    piece = jax.ShapeDtypeStruct((256, width), jnp.bfloat16)
    return pl.pallas_call(
        pieces_kernel,
        grid=(count,),
        in_specs=[
            pl.BlockSpec((256, depth), lambda i: (first + i, 0)),
            pl.BlockSpec((depth, width), lambda i: (0, 0)),
        ],
        out_specs=[pl.BlockSpec((256, width), lambda i: (0, 0))] * count,
        out_shape=[piece] * count,
        compiler_params=pltpu.CompilerParams(vmem_limit_bytes=16 * 1024 * 1024),
        cost_estimate=pl.CostEstimate(flops=1, bytes_accessed=1, transcendentals=0),
    )(matrix, part)


def shards(
    coef_occ,
    coef_resp,
    orb_energy,
    lap_index,
    density_mask,
    tri_blocks,
    block_ao,
    block_slab,
    metric,
):
    row, col = lax.axis_index("row"), lax.axis_index("col")
    y, x, core = row // 2, row % 2, col % 2
    t_point = 0.04 * jnp.exp(0.5 * math.log(2.0) * lap_index[0].astype(jnp.float32))
    weighted = (coef_occ.astype(jnp.float32) * jnp.exp(t_point * orb_energy)[None, :]).astype(
        jnp.bfloat16
    )
    w_all = lax.all_gather(weighted.T, "col", axis=0, tiled=True)

    mine = coef_resp.T
    other = send(mine, flip_x)
    depth, cols_here = mine.shape
    r_all = jnp.zeros((N_ROW * depth, cols_here), mine.dtype)

    def place(r_all, part, step, xx):
        at = (((y + 4 - step) % 4) * 2 + xx) * depth
        return lax.dynamic_update_slice(r_all, part, (at, 0))

    r_all = place(r_all, mine, 0, x)
    for step in (1, 3, 2):
        r_all = place(r_all, send(mine, along_y(step)), step, x)
    r_all = place(r_all, other, 0, 1 - x)
    for step in (1, 3, 2):
        r_all = place(r_all, send(other, along_y(step)), step, 1 - x)

    table = lax.dynamic_slice(jnp.asarray(SLAB_PAIR, jnp.int32), (col, 0), (1, N_ROW))[0]
    here = 2 * jnp.asarray(ORDER)[jnp.arange(N_COL) // 2] + jnp.arange(N_COL) % 2
    pair_at = jnp.sum(
        jnp.where(
            jnp.arange(N_ROW, dtype=jnp.int32)[None, :]
            == (((y + here // 4) % 4) * 2 + (x + here // 2 % 2) % 2)[:, None],
            table[None, :],
            0,
        ),
        axis=1,
    )
    slab_at = 2 * pair_at + ((here % 2) ^ core)
    n_ao = coef_occ.shape[0] // 128
    chosen = (block_slab[0][None, None, :] == slab_at[:, None, None]) & (
        block_ao[0][None, None, :] == jnp.arange(n_ao, dtype=jnp.int32)[None, :, None]
    )
    blocks = jnp.einsum(
        "sab,bqm->saqm",
        chosen.astype(jnp.bfloat16),
        tri_blocks[0].transpose(0, 2, 1),
        preferred_element_type=jnp.float32,
    ).astype(jnp.bfloat16)
    matrix = blocks.transpose(0, 2, 1, 3).reshape(N_COL * 128, n_ao * 128)

    rows_here = coef_occ.shape[0]
    product = lax.dot_general(
        w_all, r_all, (((0,), (0,)), ((), ())), preferred_element_type=jnp.float32
    )
    masked = (
        product.reshape(n_ao, 128, cols_here // 128, 128)
        * density_mask.astype(jnp.float32)[:, None, :, None]
    )
    pseudo = masked.reshape(rows_here, cols_here).astype(jnp.bfloat16)

    after = lax.optimization_barrier
    part = pseudo
    (piece,) = pieces_of(matrix, part, 0, 1)
    high_far = send(piece, along_y(-1))
    part, piece = after((part, piece))
    (piece,) = pieces_of(matrix, part, 1, 1)
    high_up = send(piece, along_y(1))
    part, piece = after((part, piece))
    low_two, for_high, low_one, for_low, high_own, low_own = pieces_of(matrix, part, 2, 6)
    high_far, high_up = after((high_far, high_up))
    high_near = add(for_high, high_far)
    high_down = send(high_near, along_y(-1))
    low_one, low_two, high_near = after((low_one, low_two, high_near))
    low_far = send(low_two, along_y(1))
    low_down = send(low_one, along_y(-1))
    low_up = send(add(for_low, low_far), along_y(1))
    high = add(high_own, high_up, high_down)
    crossed = send(high, flip_x)
    total = [
        add(*[term[128 * j : 128 * j + 128] for term in (low_own, low_down, low_up, crossed)])
        for j in range(2)
    ]
    got = [send(total[j], owner_of(j)) for j in range(2)]
    grad = jnp.concatenate(
        [
            lax.dot_general(
                jnp.where(core == 0, got[e], got[1 - e]),
                metric,
                (((0,), (1,)), ((), ())),
                preferred_element_type=jnp.float32,
            ).astype(jnp.bfloat16)
            for e in range(2)
        ],
        axis=0,
    )
    return (pseudo, grad)


def solution(mesh):
    placed = (
        P("row", "col"),
        P("col", "row"),
        P("col"),
        P(),
        P("row", "col"),
        P("row", None, None, None),
        P("row", None),
        P("row", None),
        P("col", None),
    )
    return jax.shard_map(
        shards,
        mesh=mesh,
        in_specs=placed,
        out_specs=(P("row", "col"), P("row", "col")),
        check_vma=False,
    )
```

time: 190 us -> 182 us (0.958)
  the two profiles are of different devices: /device:TPU:29 before, /device:TPU:103 now
where the time goes in v3:
time: 182 us; the launch traced here: 181 us
  waiting for transfers between devices  73.9 us (41%)
  local copies, waits for them, and re-layouts  28.8 us (16%)
  starting transfers between devices  25.3 us (14%)
  matrix products  22.6 us (12%)
  between operations  15 us (8%)
  Pallas kernels  10.5 us (6%)
  other arithmetic  4.84 us (3%)
    ppermute x16, waiting for transfers between devices, send(): return lax.ppermute(x, BOTH, pairs)  60.7 us
    ppermute x16, starting transfers between devices, send(): return lax.ppermute(x, BOTH, pairs)  25.3 us
    dot_general x1, matrix products, shards(): lax.dot_general(w_all, r_all, (((0,), (0,)), ((), ())), preferred_element...  16.4 us
    all_gather x1, waiting for transfers between devices, shards(): w_all = lax.all_gather(weighted.T, 'col', axis=0, tiled=True)  13.2 us
    unnamed x19, local copies, waits for them, and re-layouts  11.1 us
    pallas_call x3, Pallas kernels, pieces_of(): pl.pallas_call(pieces_kernel, grid=(count,), in_specs=[pl.BlockSpec((256,...  10.5 us
    dynamic_update_slice x8, local copies, waits for them, and re-layouts, place(): return lax.dynamic_update_slice(r_all, part, (at, 0))  9.35 us
    dot_general x1, matrix products, shards(): jnp.einsum('sab,bqm->saqm', chosen.astype(jnp.bfloat16), tri_blocks[0].tr...  5.7 us
  transfers between devices with their start and end apart: 17, of which 10 were waited for; matrix products, arithmetic and copies ran while one was open for 19% of the time, Pallas kernels for 4%

profile of v3, /device:TPU:103, one launch (start us, length us, event | category | flops | bytes accessed | tf_op | source)
XLA Modules:
  0.0 180.9 jit_solution(8516430984089189864)
XLA Ops:
  8.6 2.1 %fusion.2 = bf16[160,2048]{1,0:T(8,128)(2,1)} fusion(bf16[2048,160]{0,1:T(8,128)(2,1)} %param.11, f32[160]{0:T(256)S(1)} %multiply_exponential_fusion), kind=kLoop, calls=%fused_computation.12 | loop fusion | flops 983040 | bytes 1311360 | tf_op jit(solution)/shard_map/transpose | solution.py:106
  13.6 1.6 collective-permute-start.2
  16.3 3.3 %copy.18 = bf16[64,128,128]{2,0,1:T(8,128)(2,1)S(1)} copy(bf16[64,128,128]{1,2,0:T(8,128)(2,1)} %bitcast.45) | data formatting | bytes 4194304 | tf_op jit(solution)/shard_map/transpose | solution.py:143
  21.3 5.7 %convolution_convert_fusion = bf16[16,16,128,128]{3,1,2,0:T(8,128)(2,1)} fusion(bf16[64,128,128]{2,0,1:T(8,128)(2,1)S(1)} %copy.18, pred[16,64]{1,0:T(8,128)(4,1)S(1)} %get-tuple-element.28, pred[16,64]{1,0:T(8,128)(4,1)S(1)} %get-tuple-element.29), kind=kOutput, calls=%fused_computation.4 | convolution fusion | flops 541081600 | bytes 10487808 | tf_op jit(solution)/shard_map/sab,bqm->saqm/dot_general | solution.py:140
  27.0 12.7 %collective-permute-done.3 = bf16[320,1024]{1,0:T(8,128)(2,1)S(1)} collective-permute-done((bf16[320,1024]{1,0:T(8,128)(2,1)}, bf16[320,1024]{1,0:T(8,128)(2,1)S(1)}, u32[]{:S(2)}, u32[]{:S(2)}) %collective-permute-start.3) | collective-permute-done | bytes 655392 | tf_op jit(solution)/shard_map/ppermute | solution.py:41
  39.7 2.7 %collective-permute-start.5 = (bf16[320,1024]{1,0:T(8,128)(2,1)S(1)}, bf16[320,1024]{1,0:T(8,128)(2,1)S(1)}, u32[]{:S(2)}, u32[]{:S(2)}) collective-permute-start(bf16[320,1024]{1,0:T(8,128)(2,1)S(1)} %collective-permute-done.3), channel_id=1, source_target_pairs={{0,96},{1,97},{2,98},{3,99},{4,100},{5,101},{6,102},{7,103},{8,104... | collective-permute-start | bytes 1966088 | tf_op jit(solution)/shard_map/ppermute | solution.py:41
  42.4 3.0 %broadcast_in_dim.24 = bf16[2560,1024]{1,0:T(8,128)(2,1)} broadcast(bf16[]{:T(256)} %constant.142.clone.1), dimensions={} | broadcast | bytes 5242882 | tf_op jit(solution)/shard_map/broadcast_in_dim | solution.py:111
  46.3 11.1 %copy.24 = bf16[256,8,16,128]{3,1,2,0:T(8,128)(2,1)} copy(bf16[256,8,16,128]{3,2,1,0:T(8,128)(2,1)} %bitcast.43) | data formatting | bytes 16777216
  57.4 2.0 %constant_dynamic-update-slice_fusion.6 = bf16[2560,1024]{1,0:T(8,128)(2,1)} fusion(bf16[2560,1024]{1,0:T(8,128)(2,1)} %constant_dynamic-update-slice_fusion.7, bf16[320,1024]{1,0:T(8,128)(2,1)} %collective-permute-done, s32[]{:T(128)S(6)} %select_n.169), kind=kLoop, calls=%fused_computation.37 | loop fusion | bytes 1310724 | tf_op jit(solution)/shard_map/dynamic_update_slice | solution.py:115
  59.4 2.0 %constant_dynamic-update-slice_fusion.5 = bf16[2560,1024]{1,0:T(8,128)(2,1)} fusion(bf16[2560,1024]{1,0:T(8,128)(2,1)} %constant_dynamic-update-slice_fusion.6, bf16[320,1024]{1,0:T(8,128)(2,1)} %collective-permute-done.1, s32[]{:T(128)S(6)} %select_n.171), kind=kLoop, calls=%fused_computation.36 | loop fusion | bytes 1310724 | tf_op jit(solution)/shard_map/dynamic_update_slice | solution.py:115
  65.0 3.3 %collective-permute-done.6 = bf16[320,1024]{1,0:T(8,128)(2,1)S(1)} collective-permute-done((bf16[320,1024]{1,0:T(8,128)(2,1)S(1)}, bf16[320,1024]{1,0:T(8,128)(2,1)S(1)}, u32[]{:S(2)}, u32[]{:S(2)}) %collective-permute-start.6) | collective-permute-done | bytes 655392 | tf_op jit(solution)/shard_map/ppermute | solution.py:41
  69.2 13.2 %all-gather.2.cloned.1.call-done = bf16[2560,2048]{1,0:T(8,128)(2,1)} async-done(((bf16[160,2048]{1,0:T(8,128)(2,1)}), bf16[2560,2048]{1,0:T(8,128)(2,1)}) %all-gather.2.cloned.1.call-update) | async-done | bytes 10485776 | tf_op jit(solution)/shard_map/all_gather | solution.py:106
  83.0 16.4 %fusion.part_ref = bf16[2048,1024]{1,0:T(8,128)(2,1)S(1)} fusion(f32[256,8,8,128]{3,2,1,0:T(8,128)S(1)} %bitcast.44, bf16[2560,2048]{1,0:T(8,128)(2,1)} %all-gather.2.cloned.1.call-done, bf16[2560,1024]{1,0:T(8,128)(2,1)} %constant_dynamic-update-slice_fusion), kind=kOutput, calls=%fused_computation.3 | convolution fusion | flops 10741612544 | bytes 28311552 | tf_op jit(solution)/shard_map/dot_general | solution.py:149
  102.5 2.3 %collective-permute-start.7 = (bf16[256,1024]{1,0:T(8,128)(2,1)S(1)}, bf16[256,1024]{1,0:T(8,128)(2,1)S(1)}, u32[]{:S(2)}, u32[]{:S(2)}) collective-permute-start(bf16[256,1024]{1,0:T(8,128)(2,1)S(1)} %shard_map.125), channel_id=1, source_target_pairs={{0,96},{1,97},{2,98},{3,99},{4,100},{5,101},{6,102},{7,103},{8,104... | collective-permute-start | bytes 1572872 | tf_op jit(solution)/shard_map/ppermute | solution.py:41
  104.8 8.0 %shard_map.127 = (bf16[256,1024]{1,0:T(8,128)(2,1)S(1)}, bf16[256,1024]{1,0:T(8,128)(2,1)S(1)}, bf16[256,1024]{1,0:T(8,128)(2,1)S(1)}, bf16[256,1024]{1,0:T(8,12...) custom-call(bf16[2048,2048]{1,0:T(8,128)(2,1)S(1)} %bitcast.42, ...), custom_call_target="tpu_custom_call" | custom-call | flops 1 | bytes 1 | tf_op jit(solution)/shard_map/pallas_call | solution.py:75
  112.8 3.8 %collective-permute-done.8 = bf16[256,1024]{1,0:T(8,128)(2,1)S(1)} collective-permute-done((bf16[256,1024]{1,0:T(8,128)(2,1)S(1)}, bf16[256,1024]{1,0:T(8,128)(2,1)S(1)}, u32[]{:S(2)}, u32[]{:S(2)}) %collective-permute-start.8) | collective-permute-done | bytes 524320 | tf_op jit(solution)/shard_map/ppermute | solution.py:41
  116.9 2.7 %collective-permute-start.12 = (bf16[256,1024]{1,0:T(8,128)(2,1)S(1)}, bf16[256,1024]{1,0:T(8,128)(2,1)S(1)}, u32[]{:S(2)}, u32[]{:S(2)}) collective-permute-start(bf16[256,1024]{1,0:T(8,128)(2,1)S(1)} %add_convert_fusion.2), channel_id=1, source_target_pairs={{0,96},{1,97},{2,98},{3,99},{4,100},{5,101},{6,102},{7,103},{8,104... | collective-permute-start | bytes 1572872 | tf_op jit(solution)/shard_map/ppermute | solution.py:41
  120.7 9.7 %collective-permute-done.10 = bf16[256,1024]{1,0:T(8,128)(2,1)S(1)} collective-permute-done((bf16[256,1024]{1,0:T(8,128)(2,1)S(1)}, bf16[256,1024]{1,0:T(8,128)(2,1)S(1)}, u32[]{:S(2)}, u32[]{:S(2)}) %collective-permute-start.10) | collective-permute-done | bytes 524320 | tf_op jit(solution)/shard_map/ppermute | solution.py:41
  130.9 3.4 %collective-permute-start.13 = (bf16[256,1024]{1,0:T(8,128)(2,1)S(1)}, bf16[256,1024]{1,0:T(8,128)(2,1)S(1)}, u32[]{:S(2)}, u32[]{:S(2)}) collective-permute-start(bf16[256,1024]{1,0:T(8,128)(2,1)S(1)} %add_convert_fusion), channel_id=1, source_target_pairs={{0,16},{1,17},{2,18},{3,19},{4,20},{5,21},{6,22},{7,23},{8,24},{9,... | collective-permute-start | bytes 1572872 | tf_op jit(solution)/shard_map/ppermute | solution.py:41
  134.4 6.2 %collective-permute-done.9 = bf16[256,1024]{1,0:T(8,128)(2,1)S(1)} collective-permute-done((bf16[256,1024]{1,0:T(8,128)(2,1)S(1)}, bf16[256,1024]{1,0:T(8,128)(2,1)S(1)}, u32[]{:S(2)}, u32[]{:S(2)}) %collective-permute-start.9) | collective-permute-done | bytes 524320 | tf_op jit(solution)/shard_map/ppermute | solution.py:41
  140.6 2.7 %collective-permute-done.11 = bf16[256,1024]{1,0:T(8,128)(2,1)S(1)} collective-permute-done((bf16[256,1024]{1,0:T(8,128)(2,1)S(1)}, bf16[256,1024]{1,0:T(8,128)(2,1)S(1)}, u32[]{:S(2)}, u32[]{:S(2)}) %collective-permute-start.11) | collective-permute-done | bytes 524320 | tf_op jit(solution)/shard_map/ppermute | solution.py:41
  144.2 6.8 %collective-permute-start.15 = (bf16[128,1024]{1,0:T(8,128)(2,1)S(1)}, bf16[128,1024]{1,0:T(8,128)(2,1)S(1)}, u32[]{:S(2)}, u32[]{:S(2)}) collective-permute-start(bf16[128,1024]{1,0:T(8,128)(2,1)S(1)} %get-tuple-element.27), channel_id=1, source_target_pairs={{0,7},{1,6},{2,19},{3,26},{4,37},{5,42},{6,49},{7,56},{8,73},{9,74... | collective-permute-start | bytes 786440 | tf_op jit(solution)/shard_map/ppermute | solution.py:41
  151.0 13.0 %collective-permute-done.14 = bf16[128,1024]{1,0:T(8,128)(2,1)S(1)} collective-permute-done((bf16[128,1024]{1,0:T(8,128)(2,1)S(1)}, bf16[128,1024]{1,0:T(8,128)(2,1)S(1)}, u32[]{:S(2)}, u32[]{:S(2)}) %collective-permute-start.14) | collective-permute-done | bytes 262176 | tf_op jit(solution)/shard_map/ppermute | solution.py:41
  164.0 8.7 %collective-permute-done.15 = bf16[128,1024]{1,0:T(8,128)(2,1)S(1)} collective-permute-done((bf16[128,1024]{1,0:T(8,128)(2,1)S(1)}, bf16[128,1024]{1,0:T(8,128)(2,1)S(1)}, u32[]{:S(2)}, u32[]{:S(2)}) %collective-permute-start.15) | collective-permute-done | bytes 262176 | tf_op jit(solution)/shard_map/ppermute | solution.py:41
  (66 shorter events, 19.6 us)
Async XLA Ops:
  7.2 165.5 %copy-start = (bf16[128,128]{1,0:T(8,128)(2,1)S(1)}, bf16[128,128]{1,0:T(8,128)(2,1)}, u32[]{:S(2)}) copy-start(bf16[128,128]{1,0:T(8,128)(2,1)} %param.19) | copy-start | bytes 98308
  7.2 14.0 %copy-start.6 = (s32[1,64]{1,0:T(1,128)S(1)}, s32[1,64]{1,0:T(1,128)}, u32[]{:S(2)}) copy-start(s32[1,64]{1,0:T(1,128)} %param.18) | copy-start | bytes 772
  7.2 14.0 %copy-start.5 = (s32[1,64]{1,0:T(1,128)S(1)}, s32[1,64]{1,0:T(1,128)}, u32[]{:S(2)}) copy-start(s32[1,64]{1,0:T(1,128)} %param.17) | copy-start | bytes 772
  7.2 75.2 %all-gather.2.cloned.1.call-start = ((), (), s32[]{:S(2)}) async-start(), calls=%async_computation | async-start | bytes 11141120 | tf_op jit(solution)/shard_map/all_gather | solution.py:106
  10.8 46.7 %collective-permute-start = (bf16[320,1024]{1,0:T(8,128)(2,1)}, bf16[320,1024]{1,0:T(8,128)(2,1)}, u32[]{:S(2)}, u32[]{:S(2)}) collective-permute-start(bf16[320,1024]{1,0:T(8,128)(2,1)} %bitcast.46), channel_id=1, source_target_pairs={{0,32},{1,33},{2,34},{3,35},{4,36},{5,37},{6,38},{7,39},{8,40},{9,... | collective-permute-start | bytes 1966088 | tf_op jit(solution)/shard_map/ppermute | solution.py:41
  12.1 47.3 %collective-permute-start.1 = (bf16[320,1024]{1,0:T(8,128)(2,1)}, bf16[320,1024]{1,0:T(8,128)(2,1)}, u32[]{:S(2)}, u32[]{:S(2)}) collective-permute-start(bf16[320,1024]{1,0:T(8,128)(2,1)} %bitcast.47), channel_id=1, source_target_pairs={{0,96},{1,97},{2,98},{3,99},{4,100},{5,101},{6,102},{7,103},{8,104... | collective-permute-start | bytes 1966088 | tf_op jit(solution)/shard_map/ppermute | solution.py:41
  13.6 47.8 %collective-permute-start.2 = (bf16[320,1024]{1,0:T(8,128)(2,1)}, bf16[320,1024]{1,0:T(8,128)(2,1)S(1)}, u32[]{:S(2)}, u32[]{:S(2)}) collective-permute-start(bf16[320,1024]{1,0:T(8,128)(2,1)} %bitcast.48), channel_id=1, source_target_pairs={{0,64},{1,65},{2,66},{3,67},{4,68},{5,69},{6,70},{7,71},{8,72},{9,... | collective-permute-start | bytes 1966088 | tf_op jit(solution)/shard_map/ppermute | solution.py:41
  15.2 24.5 %collective-permute-start.3 = (bf16[320,1024]{1,0:T(8,128)(2,1)}, bf16[320,1024]{1,0:T(8,128)(2,1)S(1)}, u32[]{:S(2)}, u32[]{:S(2)}) collective-permute-start(bf16[320,1024]{1,0:T(8,128)(2,1)} %bitcast.49), channel_id=1, source_target_pairs={{0,16},{1,17},{2,18},{3,19},{4,20},{5,21},{6,22},{7,23},{8,24},{9,... | collective-permute-start | bytes 1966088 | tf_op jit(solution)/shard_map/ppermute | solution.py:41
  27.0 18.4 %copy-start.3 = (bf16[1024,320]{0,1:T(8,128)(2,1)S(1)}, bf16[1024,320]{0,1:T(8,128)(2,1)}, u32[]{:S(2)}) copy-start(bf16[1024,320]{0,1:T(8,128)(2,1)} %param.12) | copy-start | bytes 1966084
  27.0 19.3 %copy-start.4 = (s32[16,8]{0,1:T(8,128)S(1)}, s32[16,8]{0,1:T(8,128)}, u32[]{:S(2)}) copy-start(s32[16,8]{0,1:T(8,128)} %param.15) | copy-start | bytes 1540
  39.7 23.5 %collective-permute-start.4 = (bf16[320,1024]{1,0:T(8,128)(2,1)S(1)}, bf16[320,1024]{1,0:T(8,128)(2,1)S(1)}, u32[]{:S(2)}, u32[]{:S(2)}) collective-permute-start(bf16[320,1024]{1,0:T(8,128)(2,1)S(1)} %collective-permute-done.3), channel_id=1, source_target_pairs={{0,32},{1,33},{2,34},{3,35},{4,36},{5,37},{6,38},{7,39},{8,40},{9,... | collective-permute-start | bytes 1966088 | tf_op jit(solution)/shard_map/ppermute | solution.py:41
  39.7 24.4 %collective-permute-start.5 = (bf16[320,1024]{1,0:T(8,128)(2,1)S(1)}, bf16[320,1024]{1,0:T(8,128)(2,1)S(1)}, u32[]{:S(2)}, u32[]{:S(2)}) collective-permute-start(bf16[320,1024]{1,0:T(8,128)(2,1)S(1)} %collective-permute-done.3), channel_id=1, source_target_pairs={{0,96},{1,97},{2,98},{3,99},{4,100},{5,101},{6,102},{7,103},{8,104... | collective-permute-start | bytes 1966088 | tf_op jit(solution)/shard_map/ppermute | solution.py:41
  57.4 10.9 %collective-permute-start.6 = (bf16[320,1024]{1,0:T(8,128)(2,1)S(1)}, bf16[320,1024]{1,0:T(8,128)(2,1)S(1)}, u32[]{:S(2)}, u32[]{:S(2)}) collective-permute-start(bf16[320,1024]{1,0:T(8,128)(2,1)S(1)} %collective-permute-done.3), channel_id=1, source_target_pairs={{0,64},{1,65},{2,66},{3,67},{4,68},{5,69},{6,70},{7,71},{8,72},{9,... | collective-permute-start | bytes 1966088 | tf_op jit(solution)/shard_map/ppermute | solution.py:41
  82.4 17.1 %slice-start = ((s8[8388608]{0:T(1024)(128)(4,1)}), s8[4194304]{0:T(1024)(128)(4,1)S(1)}, s32[]{:S(2)}) async-start(s8[8388608]{0:T(1024)(128)(4,1)} %bitcast.38), calls=%async_computation.1 | async-start | bytes 8388608
  83.0 16.5 %slice-start.1 = ((s8[8388608]{0:T(1024)(128)(4,1)}), s8[4194304]{0:T(1024)(128)(4,1)S(1)}, s32[]{:S(2)}) async-start(s8[8388608]{0:T(1024)(128)(4,1)} %bitcast.38), calls=%async_computation.2 | async-start | bytes 8388608
  102.0 14.5 %collective-permute-start.8 = (bf16[256,1024]{1,0:T(8,128)(2,1)S(1)}, bf16[256,1024]{1,0:T(8,128)(2,1)S(1)}, u32[]{:S(2)}, u32[]{:S(2)}) collective-permute-start(bf16[256,1024]{1,0:T(8,128)(2,1)S(1)} %shard_map.126), channel_id=1, source_target_pairs={{0,32},{1,33},{2,34},{3,35},{4,36},{5,37},{6,38},{7,39},{8,40},{9,... | collective-permute-start | bytes 1572872 | tf_op jit(solution)/shard_map/ppermute | solution.py:41
  102.5 14.1 %collective-permute-start.7 = (bf16[256,1024]{1,0:T(8,128)(2,1)S(1)}, bf16[256,1024]{1,0:T(8,128)(2,1)S(1)}, u32[]{:S(2)}, u32[]{:S(2)}) collective-permute-start(bf16[256,1024]{1,0:T(8,128)(2,1)S(1)} %shard_map.125), channel_id=1, source_target_pairs={{0,96},{1,97},{2,98},{3,99},{4,100},{5,101},{6,102},{7,103},{8,104... | collective-permute-start | bytes 1572872 | tf_op jit(solution)/shard_map/ppermute | solution.py:41
  116.8 13.6 %collective-permute-start.10 = (bf16[256,1024]{1,0:T(8,128)(2,1)S(1)}, bf16[256,1024]{1,0:T(8,128)(2,1)S(1)}, u32[]{:S(2)}, u32[]{:S(2)}) collective-permute-start(bf16[256,1024]{1,0:T(8,128)(2,1)S(1)} %get-tuple-element.23), channel_id=1, source_target_pairs={{0,32},{1,33},{2,34},{3,35},{4,36},{5,37},{6,38},{7,39},{8,40},{9,... | collective-permute-start | bytes 1572872 | tf_op jit(solution)/shard_map/ppermute | solution.py:41
  116.9 13.8 %collective-permute-start.12 = (bf16[256,1024]{1,0:T(8,128)(2,1)S(1)}, bf16[256,1024]{1,0:T(8,128)(2,1)S(1)}, u32[]{:S(2)}, u32[]{:S(2)}) collective-permute-start(bf16[256,1024]{1,0:T(8,128)(2,1)S(1)} %add_convert_fusion.2), channel_id=1, source_target_pairs={{0,96},{1,97},{2,98},{3,99},{4,100},{5,101},{6,102},{7,103},{8,104... | collective-permute-start | bytes 1572872 | tf_op jit(solution)/shard_map/ppermute | solution.py:41
  119.5 21.1 %collective-permute-start.9 = (bf16[256,1024]{1,0:T(8,128)(2,1)S(1)}, bf16[256,1024]{1,0:T(8,128)(2,1)S(1)}, u32[]{:S(2)}, u32[]{:S(2)}) collective-permute-start(bf16[256,1024]{1,0:T(8,128)(2,1)S(1)} %get-tuple-element.21), channel_id=1, source_target_pairs={{0,96},{1,97},{2,98},{3,99},{4,100},{5,101},{6,102},{7,103},{8,104... | collective-permute-start | bytes 1572872 | tf_op jit(solution)/shard_map/ppermute | solution.py:41
  130.6 12.7 %collective-permute-start.11 = (bf16[256,1024]{1,0:T(8,128)(2,1)S(1)}, bf16[256,1024]{1,0:T(8,128)(2,1)S(1)}, u32[]{:S(2)}, u32[]{:S(2)}) collective-permute-start(bf16[256,1024]{1,0:T(8,128)(2,1)S(1)} %add_convert_fusion.1), channel_id=1, source_target_pairs={{0,32},{1,33},{2,34},{3,35},{4,36},{5,37},{6,38},{7,39},{8,40},{9,... | collective-permute-start | bytes 1572872 | tf_op jit(solution)/shard_map/ppermute | solution.py:41
  130.9 12.8 %collective-permute-start.13 = (bf16[256,1024]{1,0:T(8,128)(2,1)S(1)}, bf16[256,1024]{1,0:T(8,128)(2,1)S(1)}, u32[]{:S(2)}, u32[]{:S(2)}) collective-permute-start(bf16[256,1024]{1,0:T(8,128)(2,1)S(1)} %add_convert_fusion), channel_id=1, source_target_pairs={{0,16},{1,17},{2,18},{3,19},{4,20},{5,21},{6,22},{7,23},{8,24},{9,... | collective-permute-start | bytes 1572872 | tf_op jit(solution)/shard_map/ppermute | solution.py:41
  144.1 19.9 %collective-permute-start.14 = (bf16[128,1024]{1,0:T(8,128)(2,1)S(1)}, bf16[128,1024]{1,0:T(8,128)(2,1)S(1)}, u32[]{:S(2)}, u32[]{:S(2)}) collective-permute-start(bf16[128,1024]{1,0:T(8,128)(2,1)S(1)} %get-tuple-element.26), channel_id=1, source_target_pairs={{0,6},{1,7},{2,18},{3,27},{4,36},{5,43},{6,48},{7,57},{8,72},{9,75... | collective-permute-start | bytes 786440 | tf_op jit(solution)/shard_map/ppermute | solution.py:41
  144.2 28.5 %collective-permute-start.15 = (bf16[128,1024]{1,0:T(8,128)(2,1)S(1)}, bf16[128,1024]{1,0:T(8,128)(2,1)S(1)}, u32[]{:S(2)}, u32[]{:S(2)}) collective-permute-start(bf16[128,1024]{1,0:T(8,128)(2,1)S(1)} %get-tuple-element.27), channel_id=1, source_target_pairs={{0,7},{1,6},{2,19},{3,26},{4,37},{5,42},{6,49},{7,56},{8,73},{9,74... | collective-permute-start | bytes 786440 | tf_op jit(solution)/shard_map/ppermute | solution.py:41
  (2 other events, 17.8 us)
Sparse Core Ops, SparseCore 0:
  10.9 71.4 all-gather.1

commit v4 on v3

--- a/solution.py
+++ b/solution.py
@@ -69,21 +69,48 @@
             out[...] = value.astype(out.dtype)
 
 
-def pieces_of(matrix, part, first, count):
+def pieces_of(matrix, part, first, count, half=None):
     depth, width = part.shape
+    if half is not None:
+        width = width // 2
+    at = half or 0
     piece = jax.ShapeDtypeStruct((256, width), jnp.bfloat16)
     return pl.pallas_call(
         pieces_kernel,
         grid=(count,),
         in_specs=[
             pl.BlockSpec((256, depth), lambda i: (first + i, 0)),
-            pl.BlockSpec((depth, width), lambda i: (0, 0)),
+            pl.BlockSpec((depth, width), lambda i: (0, at)),
         ],
         out_specs=[pl.BlockSpec((256, width), lambda i: (0, 0))] * count,
         out_shape=[piece] * count,
         compiler_params=pltpu.CompilerParams(vmem_limit_bytes=16 * 1024 * 1024),
         cost_estimate=pl.CostEstimate(flops=1, bytes_accessed=1, transcendentals=0),
     )(matrix, part)
+
+
+def weigh_kernel(lap_ref, energy_ref, coef_ref, out_ref):
+    depth = coef_ref.shape[0]
+    here = lax.broadcasted_iota(jnp.int32, (depth, depth), 0)
+    there = lax.broadcasted_iota(jnp.int32, (depth, depth), 1)
+    energy = jnp.sum(jnp.where(here == there, energy_ref[...], 0.0), axis=1, keepdims=True)
+    lap = jnp.full(energy.shape, lap_ref[0], jnp.int32).astype(jnp.float32)
+    scale = jnp.exp(0.04 * jnp.exp(0.5 * math.log(2.0) * lap) * energy)
+    out_ref[...] = (coef_ref[...].astype(jnp.float32) * scale).astype(out_ref.dtype)
+
+
+def weigh(lap_index, orb_energy, coef):
+    return pl.pallas_call(
+        weigh_kernel,
+        in_specs=[
+            pl.BlockSpec(memory_space=pltpu.SMEM),
+            pl.BlockSpec(memory_space=pltpu.VMEM),
+            pl.BlockSpec(memory_space=pltpu.VMEM),
+        ],
+        out_specs=pl.BlockSpec(memory_space=pltpu.VMEM),
+        out_shape=jax.ShapeDtypeStruct(coef.shape, jnp.bfloat16),
+        compiler_params=pltpu.CompilerParams(vmem_limit_bytes=60 * 1024 * 1024),
+    )(lap_index, orb_energy[None, :], coef)
 
 
 def shards(
@@ -99,11 +126,8 @@
 ):
     row, col = lax.axis_index("row"), lax.axis_index("col")
     y, x, core = row // 2, row % 2, col % 2
-    t_point = 0.04 * jnp.exp(0.5 * math.log(2.0) * lap_index[0].astype(jnp.float32))
-    weighted = (coef_occ.astype(jnp.float32) * jnp.exp(t_point * orb_energy)[None, :]).astype(
-        jnp.bfloat16
-    )
-    w_all = lax.all_gather(weighted.T, "col", axis=0, tiled=True)
+    weighted = weigh(lap_index, orb_energy, coef_occ.T)
+    w_all = lax.all_gather(weighted, "col", axis=0, tiled=True)
 
     mine = coef_resp.T
     other = send(mine, flip_x)
@@ -157,20 +181,41 @@
 
     after = lax.optimization_barrier
     part = pseudo
-    (piece,) = pieces_of(matrix, part, 0, 1)
-    high_far = send(piece, along_y(-1))
-    part, piece = after((part, piece))
-    (piece,) = pieces_of(matrix, part, 1, 1)
+
+    def chain(part, *args):
+        made = pieces_of(matrix, part, *args)
+        return after((part, *made))
+
+    part, piece = chain(part, 0, 1, 0)
+    high_far_a = send(piece, along_y(-1))
+    part, piece = chain(part, 0, 1, 1)
+    high_far_b = send(piece, along_y(-1))
+    part, piece = chain(part, 1, 1)
     high_up = send(piece, along_y(1))
-    part, piece = after((part, piece))
-    low_two, for_high, low_one, for_low, high_own, low_own = pieces_of(matrix, part, 2, 6)
-    high_far, high_up = after((high_far, high_up))
-    high_near = add(for_high, high_far)
-    high_down = send(high_near, along_y(-1))
-    low_one, low_two, high_near = after((low_one, low_two, high_near))
-    low_far = send(low_two, along_y(1))
+    part, piece = chain(part, 2, 1, 0)
+    low_far_a = send(piece, along_y(1))
+    part, piece = chain(part, 2, 1, 1)
+    low_far_b = send(piece, along_y(1))
+    part, for_high = chain(part, 3, 1)
+    part, low_one, for_low = chain(part, 4, 2)
+    wide = for_high.shape[1] // 2
+    high_near = add(for_high[:, :wide], high_far_a)
+    part, high_near = after((part, high_near))
+    high_down_a = send(high_near, along_y(-1))
+    high_own, low_own = pieces_of(matrix, part, 6, 2)
+    high_far_b, high_up, high_own = after((high_far_b, high_up, high_own))
+    high_near = add(for_high[:, wide:], high_far_b)
+    high_down_b = send(high_near, along_y(-1))
+    low_one, high_near, low_far_a = after((low_one, high_near, low_far_a))
     low_down = send(low_one, along_y(-1))
-    low_up = send(add(for_low, low_far), along_y(1))
+    low_near = [
+        add(for_low[:, :wide], low_far_a),
+        add(for_low[:, wide:], low_far_b),
+    ]
+    low_up = [send(part, along_y(1)) for part in low_near]
+    high_down_a, high_down_b, *low_near = after((high_down_a, high_down_b, *low_near))
+    low_up = jnp.concatenate(low_up, axis=1)
+    high_down = jnp.concatenate([high_down_a, high_down_b], axis=1)
     high = add(high_own, high_up, high_down)
     crossed = send(high, flip_x)
     total = [

time: 182 us -> 181 us (level)
  other arithmetic: 4.84 us -> 1.93 us
  Pallas kernels: 10.5 us -> 12.8 us
  waiting for transfers between devices: 73.9 us -> 71.8 us
  starting transfers between devices: 25.3 us -> 27.2 us
    ppermute x16 -> x20, waiting for transfers between devices: 60.7 us -> 58.4 us  [send(): return lax.ppermute(x, BOTH, pairs)]
    pallas_call x0 -> x1, Pallas kernels: none -> 2.15 us  [weigh(): pl.pallas_call(weigh_kernel, in_specs=[pl.BlockSpec(memory_space=pltpu.SM...]
    transpose x1 -> x0, other arithmetic: 2.1 us -> none  [shards(): w_all = lax.all_gather(weighted.T, 'col', axis=0, tiled=True)]
    ppermute x16 -> x20, starting transfers between devices: 25.3 us -> 27.2 us  [send(): return lax.ppermute(x, BOTH, pairs)]
    pallas_call x3 -> x8, Pallas kernels: 10.5 us -> 10.6 us  [pieces_of(): pl.pallas_call(pieces_kernel, grid=(count,), in_specs=[pl.BlockSpec((256,...]
    unnamed x19 -> x20, local copies, waits for them, and re-layouts: 11.1 us -> 11.2 us
  transfers between devices with their start and end apart: 17 -> 21, of which waited for: 10 -> 9; matrix products, arithmetic and copies ran while one was open for 19% -> 19% of each run, Pallas kernels for 4% -> 4%
where the time goes in v4:
time: 181 us; the launch traced here: 180 us
  waiting for transfers between devices  71.8 us (40%)
  local copies, waits for them, and re-layouts  28.8 us (16%)
  starting transfers between devices  27.2 us (15%)
  matrix products  22.6 us (12%)
  between operations  15 us (8%)
  Pallas kernels  12.8 us (7%)
  other arithmetic  1.93 us (1%)
    ppermute x20, waiting for transfers between devices, send(): return lax.ppermute(x, BOTH, pairs)  58.4 us
    ppermute x20, starting transfers between devices, send(): return lax.ppermute(x, BOTH, pairs)  27.2 us
    dot_general x1, matrix products, shards(): lax.dot_general(w_all, r_all, (((0,), (0,)), ((), ())), preferred_element...  16.4 us
    all_gather x1, waiting for transfers between devices, shards(): w_all = lax.all_gather(weighted, 'col', axis=0, tiled=True)  13.3 us
    unnamed x20, local copies, waits for them, and re-layouts  11.2 us
    pallas_call x8, Pallas kernels, pieces_of(): pl.pallas_call(pieces_kernel, grid=(count,), in_specs=[pl.BlockSpec((256,...  10.6 us
    dynamic_update_slice x8, local copies, waits for them, and re-layouts, place(): return lax.dynamic_update_slice(r_all, part, (at, 0))  9.31 us
    dot_general x1, matrix products, shards(): jnp.einsum('sab,bqm->saqm', chosen.astype(jnp.bfloat16), tri_blocks[0].tr...  5.71 us
  transfers between devices with their start and end apart: 21, of which 9 were waited for; matrix products, arithmetic and copies ran while one was open for 19% of the time, Pallas kernels for 4%

profile of v4, /device:TPU:103, one launch (start us, length us, event | category | flops | bytes accessed | tf_op | source)
XLA Modules:
  0.0 180.2 jit_solution(13703181603183483601)
XLA Ops:
  7.9 2.1 %shard_map.125 = bf16[160,2048]{1,0:T(8,128)(2,1)} custom-call(s32[1]{0:T(128)S(6)} %copy.34.lap_ref, f32[1,160]{1,0:T(1,128)} %bitcast.55, bf16[160,2048]{1,0:T(8,128)(2,1)} %bitcast.54), custom_call_target="tpu_custom_call" | custom-call | tf_op jit(solution)/shard_map/pallas_call | solution.py:103
  15.7 3.3 %copy.18 = bf16[64,128,128]{2,0,1:T(8,128)(2,1)S(1)} copy(bf16[64,128,128]{1,2,0:T(8,128)(2,1)} %bitcast.49) | data formatting | bytes 4194304 | tf_op jit(solution)/shard_map/transpose | solution.py:167
  20.6 5.7 %convolution_convert_fusion = bf16[16,16,128,128]{3,1,2,0:T(8,128)(2,1)} fusion(bf16[64,128,128]{2,0,1:T(8,128)(2,1)S(1)} %copy.18, pred[16,64]{1,0:T(8,128)(4,1)S(1)} %get-tuple-element.62, pred[16,64]{1,0:T(8,128)(4,1)S(1)} %get-tuple-element.63), kind=kOutput, calls=%fused_computation.4 | convolution fusion | flops 541081600 | bytes 10487808 | tf_op jit(solution)/shard_map/sab,bqm->saqm/dot_general | solution.py:164
  26.3 12.6 %collective-permute-done.3 = bf16[320,1024]{1,0:T(8,128)(2,1)S(1)} collective-permute-done((bf16[320,1024]{1,0:T(8,128)(2,1)}, bf16[320,1024]{1,0:T(8,128)(2,1)S(1)}, u32[]{:S(2)}, u32[]{:S(2)}) %collective-permute-start.3) | collective-permute-done | bytes 655392 | tf_op jit(solution)/shard_map/ppermute | solution.py:41
  38.9 2.7 %collective-permute-start.5 = (bf16[320,1024]{1,0:T(8,128)(2,1)S(1)}, bf16[320,1024]{1,0:T(8,128)(2,1)S(1)}, u32[]{:S(2)}, u32[]{:S(2)}) collective-permute-start(bf16[320,1024]{1,0:T(8,128)(2,1)S(1)} %collective-permute-done.3), channel_id=1, source_target_pairs={{0,96},{1,97},{2,98},{3,99},{4,100},{5,101},{6,102},{7,103},{8,104... | collective-permute-start | bytes 1966088 | tf_op jit(solution)/shard_map/ppermute | solution.py:41
  41.6 3.0 %broadcast_in_dim.27 = bf16[2560,1024]{1,0:T(8,128)(2,1)} broadcast(bf16[]{:T(256)} %constant.136.clone.1), dimensions={} | broadcast | bytes 5242882 | tf_op jit(solution)/shard_map/broadcast_in_dim | solution.py:135
  45.5 11.1 %copy.24 = bf16[256,8,16,128]{3,1,2,0:T(8,128)(2,1)} copy(bf16[256,8,16,128]{3,2,1,0:T(8,128)(2,1)} %bitcast.47) | data formatting | bytes 16777216
  56.6 2.0 %constant_dynamic-update-slice_fusion.8 = bf16[2560,1024]{1,0:T(8,128)(2,1)} fusion(bf16[2560,1024]{1,0:T(8,128)(2,1)} %constant_dynamic-update-slice_fusion.9, bf16[320,1024]{1,0:T(8,128)(2,1)} %collective-permute-done, s32[]{:T(128)S(6)} %select_n.169), kind=kLoop, calls=%fused_computation.39 | loop fusion | bytes 1310724 | tf_op jit(solution)/shard_map/dynamic_update_slice | solution.py:139
  58.6 2.0 %constant_dynamic-update-slice_fusion.7 = bf16[2560,1024]{1,0:T(8,128)(2,1)} fusion(bf16[2560,1024]{1,0:T(8,128)(2,1)} %constant_dynamic-update-slice_fusion.8, bf16[320,1024]{1,0:T(8,128)(2,1)} %collective-permute-done.1, s32[]{:T(128)S(6)} %select_n.171), kind=kLoop, calls=%fused_computation.38 | loop fusion | bytes 1310724 | tf_op jit(solution)/shard_map/dynamic_update_slice | solution.py:139
  64.2 3.4 %collective-permute-done.6 = bf16[320,1024]{1,0:T(8,128)(2,1)S(1)} collective-permute-done((bf16[320,1024]{1,0:T(8,128)(2,1)S(1)}, bf16[320,1024]{1,0:T(8,128)(2,1)S(1)}, u32[]{:S(2)}, u32[]{:S(2)}) %collective-permute-start.6) | collective-permute-done | bytes 655392 | tf_op jit(solution)/shard_map/ppermute | solution.py:41
  68.4 13.3 %all-gather.2.cloned.1.call-done = bf16[2560,2048]{1,0:T(8,128)(2,1)} async-done(((bf16[160,2048]{1,0:T(8,128)(2,1)}), bf16[2560,2048]{1,0:T(8,128)(2,1)}) %all-gather.2.cloned.1.call-update) | async-done | bytes 10485776 | tf_op jit(solution)/shard_map/all_gather | solution.py:130
  82.4 16.4 %fusion.part_ref = bf16[2048,1024]{1,0:T(8,128)(2,1)S(1)} fusion(f32[256,8,8,128]{3,2,1,0:T(8,128)S(1)} %bitcast.48, bf16[2560,2048]{1,0:T(8,128)(2,1)} %all-gather.2.cloned.1.call-done, bf16[2560,1024]{1,0:T(8,128)(2,1)} %constant_dynamic-update-slice_fusion.2), kind=kOutput, calls=%fused_computation.3 | convolution fusion | flops 10741612544 | bytes 28311552 | tf_op jit(solution)/shard_map/dot_general | solution.py:173
  102.0 2.3 %collective-permute-start.7 = (bf16[256,512]{1,0:T(8,128)(2,1)S(1)}, bf16[256,512]{1,0:T(8,128)(2,1)S(1)}, u32[]{:S(2)}, u32[]{:S(2)}) collective-permute-start(bf16[256,512]{1,0:T(8,128)(2,1)S(1)} %shard_map.126), channel_id=1, source_target_pairs={{0,96},{1,97},{2,98},{3,99},{4,100},{5,101},{6,102},{7,103},{8,104... | collective-permute-start | bytes 786440 | tf_op jit(solution)/shard_map/ppermute | solution.py:41
  107.0 2.6 %shard_map.132 = (bf16[256,1024]{1,0:T(8,128)(2,1)S(1)}, bf16[256,1024]{1,0:T(8,128)(2,1)S(1)}) custom-call(bf16[2048,2048]{1,0:T(8,128)(2,1)S(1)} %bitcast.45, bf16[2048,1024]{1,0:T(8,128)(2,1)S(1)} %fusion.part_ref), custom_call_target="tpu_custom_call" | custom-call | flops 1 | bytes 1 | tf_op jit(solution)/shard_map/pallas_call | solution.py:78
  111.5 2.6 %shard_map.133 = (bf16[256,1024]{1,0:T(8,128)(2,1)S(1)}, bf16[256,1024]{1,0:T(8,128)(2,1)S(1)}) custom-call(bf16[2048,2048]{1,0:T(8,128)(2,1)S(1)} %bitcast.46, bf16[2048,1024]{1,0:T(8,128)(2,1)S(1)} %fusion.part_ref), custom_call_target="tpu_custom_call" | custom-call | flops 1 | bytes 1 | tf_op jit(solution)/shard_map/pallas_call | solution.py:78
  114.2 2.7 %collective-permute-start.15 = (bf16[256,512]{1,0:T(8,128)(2,1)S(1)}, bf16[256,512]{1,0:T(8,128)(2,1)S(1)}, u32[]{:S(2)}, u32[]{:S(2)}) collective-permute-start(bf16[256,512]{1,0:T(8,128)(2,1)S(1)} %add_convert_fusion.6), channel_id=1, source_target_pairs={{0,96},{1,97},{2,98},{3,99},{4,100},{5,101},{6,102},{7,103},{8,104... | collective-permute-start | bytes 786440 | tf_op jit(solution)/shard_map/ppermute | solution.py:41
  118.5 3.1 %collective-permute-done.10 = bf16[256,512]{1,0:T(8,128)(2,1)S(1)} collective-permute-done((bf16[256,512]{1,0:T(8,128)(2,1)S(1)}, bf16[256,512]{1,0:T(8,128)(2,1)S(1)}, u32[]{:S(2)}, u32[]{:S(2)}) %collective-permute-start.10) | collective-permute-done | bytes 262176 | tf_op jit(solution)/shard_map/ppermute | solution.py:41
  121.7 5.6 %collective-permute-done.13 = bf16[256,512]{1,0:T(8,128)(2,1)S(1)} collective-permute-done((bf16[256,512]{1,0:T(8,128)(2,1)S(1)}, bf16[256,512]{1,0:T(8,128)(2,1)S(1)}, u32[]{:S(2)}, u32[]{:S(2)}) %collective-permute-start.13) | collective-permute-done | bytes 262176 | tf_op jit(solution)/shard_map/ppermute | solution.py:41
  127.7 3.4 %collective-permute-start.17 = (bf16[256,1024]{1,0:T(8,128)(2,1)S(1)}, bf16[256,1024]{1,0:T(8,128)(2,1)S(1)}, u32[]{:S(2)}, u32[]{:S(2)}) collective-permute-start(bf16[256,1024]{1,0:T(8,128)(2,1)S(1)} %add_convert_fusion), channel_id=1, source_target_pairs={{0,16},{1,17},{2,18},{3,19},{4,20},{5,21},{6,22},{7,23},{8,24},{9,... | collective-permute-start | bytes 1572872 | tf_op jit(solution)/shard_map/ppermute | solution.py:41
  132.0 5.9 %collective-permute-done.12 = bf16[256,512]{1,0:T(8,128)(2,1)S(1)} collective-permute-done((bf16[256,512]{1,0:T(8,128)(2,1)S(1)}, bf16[256,512]{1,0:T(8,128)(2,1)S(1)}, u32[]{:S(2)}, u32[]{:S(2)}) %collective-permute-start.12) | collective-permute-done | bytes 262176 | tf_op jit(solution)/shard_map/ppermute | solution.py:41
  137.9 3.4 %collective-permute-done.14 = bf16[256,512]{1,0:T(8,128)(2,1)S(1)} collective-permute-done((bf16[256,512]{1,0:T(8,128)(2,1)S(1)}, bf16[256,512]{1,0:T(8,128)(2,1)S(1)}, u32[]{:S(2)}, u32[]{:S(2)}) %collective-permute-start.14) | collective-permute-done | bytes 262176 | tf_op jit(solution)/shard_map/ppermute | solution.py:41
  141.7 5.7 %collective-permute-start.19 = (bf16[128,1024]{1,0:T(8,128)(2,1)S(1)}, bf16[128,1024]{1,0:T(8,128)(2,1)S(1)}, u32[]{:S(2)}, u32[]{:S(2)}) collective-permute-start(bf16[128,1024]{1,0:T(8,128)(2,1)S(1)} %get-tuple-element.59), channel_id=1, source_target_pairs={{0,7},{1,6},{2,19},{3,26},{4,37},{5,42},{6,49},{7,56},{8,73},{9,74... | collective-permute-start | bytes 786440 | tf_op jit(solution)/shard_map/ppermute | solution.py:41
  147.5 13.3 %collective-permute-done.18 = bf16[128,1024]{1,0:T(8,128)(2,1)S(1)} collective-permute-done((bf16[128,1024]{1,0:T(8,128)(2,1)S(1)}, bf16[128,1024]{1,0:T(8,128)(2,1)S(1)}, u32[]{:S(2)}, u32[]{:S(2)}) %collective-permute-start.18) | collective-permute-done | bytes 262176 | tf_op jit(solution)/shard_map/ppermute | solution.py:41
  160.7 11.2 %collective-permute-done.19 = bf16[128,1024]{1,0:T(8,128)(2,1)S(1)} collective-permute-done((bf16[128,1024]{1,0:T(8,128)(2,1)S(1)}, bf16[128,1024]{1,0:T(8,128)(2,1)S(1)}, u32[]{:S(2)}, u32[]{:S(2)}) %collective-permute-start.19) | collective-permute-done | bytes 262176 | tf_op jit(solution)/shard_map/ppermute | solution.py:41
  (81 shorter events, 25.7 us)
Async XLA Ops:
  7.2 164.8 %copy-start = (bf16[128,128]{1,0:T(8,128)(2,1)S(1)}, bf16[128,128]{1,0:T(8,128)(2,1)}, u32[]{:S(2)}) copy-start(bf16[128,128]{1,0:T(8,128)(2,1)} %param.19) | copy-start | bytes 98308
  7.2 74.5 %all-gather.2.cloned.1.call-start = ((), (), s32[]{:S(2)}) async-start(), calls=%async_computation | async-start | bytes 11141120 | tf_op jit(solution)/shard_map/all_gather | solution.py:130
  10.1 46.5 %collective-permute-start = (bf16[320,1024]{1,0:T(8,128)(2,1)}, bf16[320,1024]{1,0:T(8,128)(2,1)}, u32[]{:S(2)}, u32[]{:S(2)}) collective-permute-start(bf16[320,1024]{1,0:T(8,128)(2,1)} %bitcast.50), channel_id=1, source_target_pairs={{0,32},{1,33},{2,34},{3,35},{4,36},{5,37},{6,38},{7,39},{8,40},{9,... | collective-permute-start | bytes 1966088 | tf_op jit(solution)/shard_map/ppermute | solution.py:41
  11.4 47.1 %collective-permute-start.1 = (bf16[320,1024]{1,0:T(8,128)(2,1)}, bf16[320,1024]{1,0:T(8,128)(2,1)}, u32[]{:S(2)}, u32[]{:S(2)}) collective-permute-start(bf16[320,1024]{1,0:T(8,128)(2,1)} %bitcast.51), channel_id=1, source_target_pairs={{0,96},{1,97},{2,98},{3,99},{4,100},{5,101},{6,102},{7,103},{8,104... | collective-permute-start | bytes 1966088 | tf_op jit(solution)/shard_map/ppermute | solution.py:41
  13.0 47.6 %collective-permute-start.2 = (bf16[320,1024]{1,0:T(8,128)(2,1)}, bf16[320,1024]{1,0:T(8,128)(2,1)S(1)}, u32[]{:S(2)}, u32[]{:S(2)}) collective-permute-start(bf16[320,1024]{1,0:T(8,128)(2,1)} %bitcast.52), channel_id=1, source_target_pairs={{0,64},{1,65},{2,66},{3,67},{4,68},{5,69},{6,70},{7,71},{8,72},{9,... | collective-permute-start | bytes 1966088 | tf_op jit(solution)/shard_map/ppermute | solution.py:41
  14.5 24.4 %collective-permute-start.3 = (bf16[320,1024]{1,0:T(8,128)(2,1)}, bf16[320,1024]{1,0:T(8,128)(2,1)S(1)}, u32[]{:S(2)}, u32[]{:S(2)}) collective-permute-start(bf16[320,1024]{1,0:T(8,128)(2,1)} %bitcast.53), channel_id=1, source_target_pairs={{0,16},{1,17},{2,18},{3,19},{4,20},{5,21},{6,22},{7,23},{8,24},{9,... | collective-permute-start | bytes 1966088 | tf_op jit(solution)/shard_map/ppermute | solution.py:41
  26.3 18.3 %copy-start.3 = (bf16[1024,320]{0,1:T(8,128)(2,1)S(1)}, bf16[1024,320]{0,1:T(8,128)(2,1)}, u32[]{:S(2)}) copy-start(bf16[1024,320]{0,1:T(8,128)(2,1)} %param.12) | copy-start | bytes 1966084
  26.3 19.1 %copy-start.4 = (s32[16,8]{0,1:T(8,128)S(1)}, s32[16,8]{0,1:T(8,128)}, u32[]{:S(2)}) copy-start(s32[16,8]{0,1:T(8,128)} %param.15) | copy-start | bytes 1540
  38.9 23.5 %collective-permute-start.4 = (bf16[320,1024]{1,0:T(8,128)(2,1)S(1)}, bf16[320,1024]{1,0:T(8,128)(2,1)S(1)}, u32[]{:S(2)}, u32[]{:S(2)}) collective-permute-start(bf16[320,1024]{1,0:T(8,128)(2,1)S(1)} %collective-permute-done.3), channel_id=1, source_target_pairs={{0,32},{1,33},{2,34},{3,35},{4,36},{5,37},{6,38},{7,39},{8,40},{9,... | collective-permute-start | bytes 1966088 | tf_op jit(solution)/shard_map/ppermute | solution.py:41
  38.9 24.4 %collective-permute-start.5 = (bf16[320,1024]{1,0:T(8,128)(2,1)S(1)}, bf16[320,1024]{1,0:T(8,128)(2,1)S(1)}, u32[]{:S(2)}, u32[]{:S(2)}) collective-permute-start(bf16[320,1024]{1,0:T(8,128)(2,1)S(1)} %collective-permute-done.3), channel_id=1, source_target_pairs={{0,96},{1,97},{2,98},{3,99},{4,100},{5,101},{6,102},{7,103},{8,104... | collective-permute-start | bytes 1966088 | tf_op jit(solution)/shard_map/ppermute | solution.py:41
  56.6 10.9 %collective-permute-start.6 = (bf16[320,1024]{1,0:T(8,128)(2,1)S(1)}, bf16[320,1024]{1,0:T(8,128)(2,1)S(1)}, u32[]{:S(2)}, u32[]{:S(2)}) collective-permute-start(bf16[320,1024]{1,0:T(8,128)(2,1)S(1)} %collective-permute-done.3), channel_id=1, source_target_pairs={{0,64},{1,65},{2,66},{3,67},{4,68},{5,69},{6,70},{7,71},{8,72},{9,... | collective-permute-start | bytes 1966088 | tf_op jit(solution)/shard_map/ppermute | solution.py:41
  101.5 15.4 %collective-permute-start.9 = (bf16[256,1024]{1,0:T(8,128)(2,1)S(1)}, bf16[256,1024]{1,0:T(8,128)(2,1)S(1)}, u32[]{:S(2)}, u32[]{:S(2)}) collective-permute-start(bf16[256,1024]{1,0:T(8,128)(2,1)S(1)} %shard_map.128), channel_id=1, source_target_pairs={{0,32},{1,33},{2,34},{3,35},{4,36},{5,37},{6,38},{7,39},{8,40},{9,... | collective-permute-start | bytes 1572872 | tf_op jit(solution)/shard_map/ppermute | solution.py:41
  102.0 9.5 %collective-permute-start.7 = (bf16[256,512]{1,0:T(8,128)(2,1)S(1)}, bf16[256,512]{1,0:T(8,128)(2,1)S(1)}, u32[]{:S(2)}, u32[]{:S(2)}) collective-permute-start(bf16[256,512]{1,0:T(8,128)(2,1)S(1)} %shard_map.126), channel_id=1, source_target_pairs={{0,96},{1,97},{2,98},{3,99},{4,100},{5,101},{6,102},{7,103},{8,104... | collective-permute-start | bytes 786440 | tf_op jit(solution)/shard_map/ppermute | solution.py:41
  104.3 12.6 %collective-permute-start.8 = (bf16[256,512]{1,0:T(8,128)(2,1)S(1)}, bf16[256,512]{1,0:T(8,128)(2,1)S(1)}, u32[]{:S(2)}, u32[]{:S(2)}) collective-permute-start(bf16[256,512]{1,0:T(8,128)(2,1)S(1)} %shard_map.127), channel_id=1, source_target_pairs={{0,96},{1,97},{2,98},{3,99},{4,100},{5,101},{6,102},{7,103},{8,104... | collective-permute-start | bytes 786440 | tf_op jit(solution)/shard_map/ppermute | solution.py:41
  109.6 12.0 %collective-permute-start.10 = (bf16[256,512]{1,0:T(8,128)(2,1)S(1)}, bf16[256,512]{1,0:T(8,128)(2,1)S(1)}, u32[]{:S(2)}, u32[]{:S(2)}) collective-permute-start(bf16[256,512]{1,0:T(8,128)(2,1)S(1)} %shard_map.129), channel_id=1, source_target_pairs={{0,32},{1,33},{2,34},{3,35},{4,36},{5,37},{6,38},{7,39},{8,40},{9,... | collective-permute-start | bytes 786440 | tf_op jit(solution)/shard_map/ppermute | solution.py:41
  111.4 15.9 %collective-permute-start.13 = (bf16[256,512]{1,0:T(8,128)(2,1)S(1)}, bf16[256,512]{1,0:T(8,128)(2,1)S(1)}, u32[]{:S(2)}, u32[]{:S(2)}) collective-permute-start(bf16[256,512]{1,0:T(8,128)(2,1)S(1)} %shard_map.130), channel_id=1, source_target_pairs={{0,32},{1,33},{2,34},{3,35},{4,36},{5,37},{6,38},{7,39},{8,40},{9,... | collective-permute-start | bytes 786440 | tf_op jit(solution)/shard_map/ppermute | solution.py:41
  114.2 13.2 %collective-permute-start.15 = (bf16[256,512]{1,0:T(8,128)(2,1)S(1)}, bf16[256,512]{1,0:T(8,128)(2,1)S(1)}, u32[]{:S(2)}, u32[]{:S(2)}) collective-permute-start(bf16[256,512]{1,0:T(8,128)(2,1)S(1)} %add_convert_fusion.6), channel_id=1, source_target_pairs={{0,96},{1,97},{2,98},{3,99},{4,100},{5,101},{6,102},{7,103},{8,104... | collective-permute-start | bytes 786440 | tf_op jit(solution)/shard_map/ppermute | solution.py:41
  117.0 10.5 %collective-permute-start.16 = (bf16[256,512]{1,0:T(8,128)(2,1)S(1)}, bf16[256,512]{1,0:T(8,128)(2,1)S(1)}, u32[]{:S(2)}, u32[]{:S(2)}) collective-permute-start(bf16[256,512]{1,0:T(8,128)(2,1)S(1)} %add_convert_fusion.5), channel_id=1, source_target_pairs={{0,96},{1,97},{2,98},{3,99},{4,100},{5,101},{6,102},{7,103},{8,104... | collective-permute-start | bytes 786440 | tf_op jit(solution)/shard_map/ppermute | solution.py:41
  121.7 19.6 %collective-permute-start.11 = (bf16[256,1024]{1,0:T(8,128)(2,1)S(1)}, bf16[256,1024]{1,0:T(8,128)(2,1)S(1)}, u32[]{:S(2)}, u32[]{:S(2)}) collective-permute-start(bf16[256,1024]{1,0:T(8,128)(2,1)S(1)} %get-tuple-element.49), channel_id=1, source_target_pairs={{0,96},{1,97},{2,98},{3,99},{4,100},{5,101},{6,102},{7,103},{8,104... | collective-permute-start | bytes 1572872 | tf_op jit(solution)/shard_map/ppermute | solution.py:41
  127.7 13.6 %collective-permute-start.17 = (bf16[256,1024]{1,0:T(8,128)(2,1)S(1)}, bf16[256,1024]{1,0:T(8,128)(2,1)S(1)}, u32[]{:S(2)}, u32[]{:S(2)}) collective-permute-start(bf16[256,1024]{1,0:T(8,128)(2,1)S(1)} %add_convert_fusion), channel_id=1, source_target_pairs={{0,16},{1,17},{2,18},{3,19},{4,20},{5,21},{6,22},{7,23},{8,24},{9,... | collective-permute-start | bytes 1572872 | tf_op jit(solution)/shard_map/ppermute | solution.py:41
  131.1 6.7 %collective-permute-start.12 = (bf16[256,512]{1,0:T(8,128)(2,1)S(1)}, bf16[256,512]{1,0:T(8,128)(2,1)S(1)}, u32[]{:S(2)}, u32[]{:S(2)}) collective-permute-start(bf16[256,512]{1,0:T(8,128)(2,1)S(1)} %get-tuple-element.61), channel_id=1, source_target_pairs={{0,32},{1,33},{2,34},{3,35},{4,36},{5,37},{6,38},{7,39},{8,40},{9,... | collective-permute-start | bytes 786440 | tf_op jit(solution)/shard_map/ppermute | solution.py:41
  131.1 10.1 %collective-permute-start.14 = (bf16[256,512]{1,0:T(8,128)(2,1)S(1)}, bf16[256,512]{1,0:T(8,128)(2,1)S(1)}, u32[]{:S(2)}, u32[]{:S(2)}) collective-permute-start(bf16[256,512]{1,0:T(8,128)(2,1)S(1)} %get-tuple-element.60), channel_id=1, source_target_pairs={{0,32},{1,33},{2,34},{3,35},{4,36},{5,37},{6,38},{7,39},{8,40},{9,... | collective-permute-start | bytes 786440 | tf_op jit(solution)/shard_map/ppermute | solution.py:41
  141.7 19.1 %collective-permute-start.18 = (bf16[128,1024]{1,0:T(8,128)(2,1)S(1)}, bf16[128,1024]{1,0:T(8,128)(2,1)S(1)}, u32[]{:S(2)}, u32[]{:S(2)}) collective-permute-start(bf16[128,1024]{1,0:T(8,128)(2,1)S(1)} %get-tuple-element.58), channel_id=1, source_target_pairs={{0,6},{1,7},{2,18},{3,27},{4,36},{5,43},{6,48},{7,57},{8,72},{9,75... | collective-permute-start | bytes 786440 | tf_op jit(solution)/shard_map/ppermute | solution.py:41
  141.7 30.2 %collective-permute-start.19 = (bf16[128,1024]{1,0:T(8,128)(2,1)S(1)}, bf16[128,1024]{1,0:T(8,128)(2,1)S(1)}, u32[]{:S(2)}, u32[]{:S(2)}) collective-permute-start(bf16[128,1024]{1,0:T(8,128)(2,1)S(1)} %get-tuple-element.59), channel_id=1, source_target_pairs={{0,7},{1,6},{2,19},{3,26},{4,37},{5,42},{6,49},{7,56},{8,73},{9,74... | collective-permute-start | bytes 786440 | tf_op jit(solution)/shard_map/ppermute | solution.py:41
  (6 other events, 84.7 us)
Sparse Core Ops, SparseCore 0:
  10.3 71.3 all-gather.1

commit v5 on v4

--- a/solution.py
+++ b/solution.py
@@ -170,14 +170,13 @@
     matrix = blocks.transpose(0, 2, 1, 3).reshape(N_COL * 128, n_ao * 128)
 
     rows_here = coef_occ.shape[0]
+    mask = jnp.broadcast_to(
+        density_mask.astype(jnp.bfloat16)[:, None, :, None], (n_ao, 128, cols_here // 128, 128)
+    ).reshape(rows_here, cols_here)
     product = lax.dot_general(
         w_all, r_all, (((0,), (0,)), ((), ())), preferred_element_type=jnp.float32
     )
-    masked = (
-        product.reshape(n_ao, 128, cols_here // 128, 128)
-        * density_mask.astype(jnp.float32)[:, None, :, None]
-    )
-    pseudo = masked.reshape(rows_here, cols_here).astype(jnp.bfloat16)
+    pseudo = (product * mask.astype(jnp.float32)).astype(jnp.bfloat16)
 
     after = lax.optimization_barrier
     part = pseudo

time: 181 us -> 181 us (level)
    ppermute x20, waiting for transfers between devices: 58.4 us -> 55.6 us  [send(): return lax.ppermute(x, BOTH, pairs)]
    all_gather x1, waiting for transfers between devices: 13.3 us -> 16.1 us  [shards(): w_all = lax.all_gather(weighted, 'col', axis=0, tiled=True)]
where the time goes in v5:
time: 181 us; the launch traced here: 180 us
  waiting for transfers between devices  71.7 us (40%)
  local copies, waits for them, and re-layouts  28.9 us (16%)
  starting transfers between devices  27.2 us (15%)
  matrix products  22.6 us (12%)
  between operations  15 us (8%)
  Pallas kernels  12.8 us (7%)
  other arithmetic  1.93 us (1%)
    ppermute x20, waiting for transfers between devices, send(): return lax.ppermute(x, BOTH, pairs)  55.6 us
    ppermute x20, starting transfers between devices, send(): return lax.ppermute(x, BOTH, pairs)  27.2 us
    dot_general x1, matrix products, shards(): lax.dot_general(w_all, r_all, (((0,), (0,)), ((), ())), preferred_element...  16.4 us
    all_gather x1, waiting for transfers between devices, shards(): w_all = lax.all_gather(weighted, 'col', axis=0, tiled=True)  16.1 us
    unnamed x20, local copies, waits for them, and re-layouts  11.2 us
    pallas_call x8, Pallas kernels, pieces_of(): pl.pallas_call(pieces_kernel, grid=(count,), in_specs=[pl.BlockSpec((256,...  10.6 us
    dynamic_update_slice x8, local copies, waits for them, and re-layouts, place(): return lax.dynamic_update_slice(r_all, part, (at, 0))  9.32 us
    dot_general x1, matrix products, shards(): jnp.einsum('sab,bqm->saqm', chosen.astype(jnp.bfloat16), tri_blocks[0].tr...  5.71 us
  transfers between devices with their start and end apart: 21, of which 9 were waited for; matrix products, arithmetic and copies ran while one was open for 19% of the time, Pallas kernels for 4%

profile of v5, /device:TPU:103, one launch (start us, length us, event | category | flops | bytes accessed | tf_op | source)
XLA Modules:
  0.0 180.2 jit_solution(11077026691506349197)
XLA Ops:
  7.9 2.1 %shard_map.125 = bf16[160,2048]{1,0:T(8,128)(2,1)} custom-call(s32[1]{0:T(128)S(6)} %copy.34.lap_ref, f32[1,160]{1,0:T(1,128)} %bitcast.55, bf16[160,2048]{1,0:T(8,128)(2,1)} %bitcast.54), custom_call_target="tpu_custom_call" | custom-call | tf_op jit(solution)/shard_map/pallas_call | solution.py:103
  15.7 3.3 %copy.18 = bf16[64,128,128]{2,0,1:T(8,128)(2,1)S(1)} copy(bf16[64,128,128]{1,2,0:T(8,128)(2,1)} %bitcast.49) | data formatting | bytes 4194304 | tf_op jit(solution)/shard_map/transpose | solution.py:167
  20.6 5.7 %convolution_convert_fusion = bf16[16,16,128,128]{3,1,2,0:T(8,128)(2,1)} fusion(bf16[64,128,128]{2,0,1:T(8,128)(2,1)S(1)} %copy.18, pred[16,64]{1,0:T(8,128)(4,1)S(1)} %get-tuple-element.62, pred[16,64]{1,0:T(8,128)(4,1)S(1)} %get-tuple-element.63), kind=kOutput, calls=%fused_computation.4 | convolution fusion | flops 541081600 | bytes 10487808 | tf_op jit(solution)/shard_map/sab,bqm->saqm/dot_general | solution.py:164
  26.3 3.0 %broadcast_in_dim.32 = bf16[2560,1024]{1,0:T(8,128)(2,1)} broadcast(bf16[]{:T(256)} %constant.136.clone.1), dimensions={} | broadcast | bytes 5242882 | tf_op jit(solution)/shard_map/broadcast_in_dim | solution.py:135
  30.2 8.7 %collective-permute-done.3 = bf16[320,1024]{1,0:T(8,128)(2,1)S(1)} collective-permute-done((bf16[320,1024]{1,0:T(8,128)(2,1)}, bf16[320,1024]{1,0:T(8,128)(2,1)S(1)}, u32[]{:S(2)}, u32[]{:S(2)}) %collective-permute-start.3) | collective-permute-done | bytes 655392 | tf_op jit(solution)/shard_map/ppermute | solution.py:41
  38.9 2.7 %collective-permute-start.5 = (bf16[320,1024]{1,0:T(8,128)(2,1)S(1)}, bf16[320,1024]{1,0:T(8,128)(2,1)S(1)}, u32[]{:S(2)}, u32[]{:S(2)}) collective-permute-start(bf16[320,1024]{1,0:T(8,128)(2,1)S(1)} %collective-permute-done.3), channel_id=1, source_target_pairs={{0,96},{1,97},{2,98},{3,99},{4,100},{5,101},{6,102},{7,103},{8,104... | collective-permute-start | bytes 1966088 | tf_op jit(solution)/shard_map/ppermute | solution.py:41
  41.6 11.2 %copy.24 = bf16[256,8,16,128]{3,1,2,0:T(8,128)(2,1)} copy(bf16[256,8,16,128]{3,2,1,0:T(8,128)(2,1)} %bitcast.47) | data formatting | bytes 16777216
  52.8 2.0 %constant_dynamic-update-slice_fusion.8 = bf16[2560,1024]{1,0:T(8,128)(2,1)} fusion(bf16[2560,1024]{1,0:T(8,128)(2,1)} %constant_dynamic-update-slice_fusion.9, bf16[320,1024]{1,0:T(8,128)(2,1)} %collective-permute-done, s32[]{:T(128)S(6)} %select_n.169), kind=kLoop, calls=%fused_computation.39 | loop fusion | bytes 1310724 | tf_op jit(solution)/shard_map/dynamic_update_slice | solution.py:139
  54.8 2.0 %constant_dynamic-update-slice_fusion.7 = bf16[2560,1024]{1,0:T(8,128)(2,1)} fusion(bf16[2560,1024]{1,0:T(8,128)(2,1)} %constant_dynamic-update-slice_fusion.8, bf16[320,1024]{1,0:T(8,128)(2,1)} %collective-permute-done.1, s32[]{:T(128)S(6)} %select_n.171), kind=kLoop, calls=%fused_computation.38 | loop fusion | bytes 1310724 | tf_op jit(solution)/shard_map/dynamic_update_slice | solution.py:139
  60.4 4.3 %collective-permute-done.6 = bf16[320,1024]{1,0:T(8,128)(2,1)S(1)} collective-permute-done((bf16[320,1024]{1,0:T(8,128)(2,1)S(1)}, bf16[320,1024]{1,0:T(8,128)(2,1)S(1)}, u32[]{:S(2)}, u32[]{:S(2)}) %collective-permute-start.6) | collective-permute-done | bytes 655392 | tf_op jit(solution)/shard_map/ppermute | solution.py:41
  65.6 16.1 %all-gather.2.cloned.1.call-done = bf16[2560,2048]{1,0:T(8,128)(2,1)} async-done(((bf16[160,2048]{1,0:T(8,128)(2,1)}), bf16[2560,2048]{1,0:T(8,128)(2,1)}) %all-gather.2.cloned.1.call-update) | async-done | bytes 10485776 | tf_op jit(solution)/shard_map/all_gather | solution.py:130
  82.4 16.4 %fusion.part_ref = bf16[2048,1024]{1,0:T(8,128)(2,1)S(1)} fusion(f32[256,8,8,128]{3,2,1,0:T(8,128)S(1)} %bitcast.48, bf16[2560,2048]{1,0:T(8,128)(2,1)} %all-gather.2.cloned.1.call-done, bf16[2560,1024]{1,0:T(8,128)(2,1)} %constant_dynamic-update-slice_fusion.2), kind=kOutput, calls=%fused_computation.3 | convolution fusion | flops 10741612544 | bytes 28311552 | tf_op jit(solution)/shard_map/dot_general | solution.py:176
  102.0 2.3 %collective-permute-start.7 = (bf16[256,512]{1,0:T(8,128)(2,1)S(1)}, bf16[256,512]{1,0:T(8,128)(2,1)S(1)}, u32[]{:S(2)}, u32[]{:S(2)}) collective-permute-start(bf16[256,512]{1,0:T(8,128)(2,1)S(1)} %shard_map.126), channel_id=1, source_target_pairs={{0,96},{1,97},{2,98},{3,99},{4,100},{5,101},{6,102},{7,103},{8,104... | collective-permute-start | bytes 786440 | tf_op jit(solution)/shard_map/ppermute | solution.py:41
  107.0 2.6 %shard_map.132 = (bf16[256,1024]{1,0:T(8,128)(2,1)S(1)}, bf16[256,1024]{1,0:T(8,128)(2,1)S(1)}) custom-call(bf16[2048,2048]{1,0:T(8,128)(2,1)S(1)} %bitcast.45, bf16[2048,1024]{1,0:T(8,128)(2,1)S(1)} %fusion.part_ref), custom_call_target="tpu_custom_call" | custom-call | flops 1 | bytes 1 | tf_op jit(solution)/shard_map/pallas_call | solution.py:78
  111.5 2.6 %shard_map.133 = (bf16[256,1024]{1,0:T(8,128)(2,1)S(1)}, bf16[256,1024]{1,0:T(8,128)(2,1)S(1)}) custom-call(bf16[2048,2048]{1,0:T(8,128)(2,1)S(1)} %bitcast.46, bf16[2048,1024]{1,0:T(8,128)(2,1)S(1)} %fusion.part_ref), custom_call_target="tpu_custom_call" | custom-call | flops 1 | bytes 1 | tf_op jit(solution)/shard_map/pallas_call | solution.py:78
  114.2 2.7 %collective-permute-start.15 = (bf16[256,512]{1,0:T(8,128)(2,1)S(1)}, bf16[256,512]{1,0:T(8,128)(2,1)S(1)}, u32[]{:S(2)}, u32[]{:S(2)}) collective-permute-start(bf16[256,512]{1,0:T(8,128)(2,1)S(1)} %add_convert_fusion.6), channel_id=1, source_target_pairs={{0,96},{1,97},{2,98},{3,99},{4,100},{5,101},{6,102},{7,103},{8,104... | collective-permute-start | bytes 786440 | tf_op jit(solution)/shard_map/ppermute | solution.py:41
  118.5 3.1 %collective-permute-done.10 = bf16[256,512]{1,0:T(8,128)(2,1)S(1)} collective-permute-done((bf16[256,512]{1,0:T(8,128)(2,1)S(1)}, bf16[256,512]{1,0:T(8,128)(2,1)S(1)}, u32[]{:S(2)}, u32[]{:S(2)}) %collective-permute-start.10) | collective-permute-done | bytes 262176 | tf_op jit(solution)/shard_map/ppermute | solution.py:41
  121.7 5.6 %collective-permute-done.13 = bf16[256,512]{1,0:T(8,128)(2,1)S(1)} collective-permute-done((bf16[256,512]{1,0:T(8,128)(2,1)S(1)}, bf16[256,512]{1,0:T(8,128)(2,1)S(1)}, u32[]{:S(2)}, u32[]{:S(2)}) %collective-permute-start.13) | collective-permute-done | bytes 262176 | tf_op jit(solution)/shard_map/ppermute | solution.py:41
  127.7 3.4 %collective-permute-start.17 = (bf16[256,1024]{1,0:T(8,128)(2,1)S(1)}, bf16[256,1024]{1,0:T(8,128)(2,1)S(1)}, u32[]{:S(2)}, u32[]{:S(2)}) collective-permute-start(bf16[256,1024]{1,0:T(8,128)(2,1)S(1)} %add_convert_fusion), channel_id=1, source_target_pairs={{0,16},{1,17},{2,18},{3,19},{4,20},{5,21},{6,22},{7,23},{8,24},{9,... | collective-permute-start | bytes 1572872 | tf_op jit(solution)/shard_map/ppermute | solution.py:41
  132.0 5.9 %collective-permute-done.12 = bf16[256,512]{1,0:T(8,128)(2,1)S(1)} collective-permute-done((bf16[256,512]{1,0:T(8,128)(2,1)S(1)}, bf16[256,512]{1,0:T(8,128)(2,1)S(1)}, u32[]{:S(2)}, u32[]{:S(2)}) %collective-permute-start.12) | collective-permute-done | bytes 262176 | tf_op jit(solution)/shard_map/ppermute | solution.py:41
  137.9 3.4 %collective-permute-done.14 = bf16[256,512]{1,0:T(8,128)(2,1)S(1)} collective-permute-done((bf16[256,512]{1,0:T(8,128)(2,1)S(1)}, bf16[256,512]{1,0:T(8,128)(2,1)S(1)}, u32[]{:S(2)}, u32[]{:S(2)}) %collective-permute-start.14) | collective-permute-done | bytes 262176 | tf_op jit(solution)/shard_map/ppermute | solution.py:41
  141.7 5.7 %collective-permute-start.19 = (bf16[128,1024]{1,0:T(8,128)(2,1)S(1)}, bf16[128,1024]{1,0:T(8,128)(2,1)S(1)}, u32[]{:S(2)}, u32[]{:S(2)}) collective-permute-start(bf16[128,1024]{1,0:T(8,128)(2,1)S(1)} %get-tuple-element.59), channel_id=1, source_target_pairs={{0,7},{1,6},{2,19},{3,26},{4,37},{5,42},{6,49},{7,56},{8,73},{9,74... | collective-permute-start | bytes 786440 | tf_op jit(solution)/shard_map/ppermute | solution.py:41
  147.5 13.3 %collective-permute-done.18 = bf16[128,1024]{1,0:T(8,128)(2,1)S(1)} collective-permute-done((bf16[128,1024]{1,0:T(8,128)(2,1)S(1)}, bf16[128,1024]{1,0:T(8,128)(2,1)S(1)}, u32[]{:S(2)}, u32[]{:S(2)}) %collective-permute-start.18) | collective-permute-done | bytes 262176 | tf_op jit(solution)/shard_map/ppermute | solution.py:41
  160.7 11.2 %collective-permute-done.19 = bf16[128,1024]{1,0:T(8,128)(2,1)S(1)} collective-permute-done((bf16[128,1024]{1,0:T(8,128)(2,1)S(1)}, bf16[128,1024]{1,0:T(8,128)(2,1)S(1)}, u32[]{:S(2)}, u32[]{:S(2)}) %collective-permute-start.19) | collective-permute-done | bytes 262176 | tf_op jit(solution)/shard_map/ppermute | solution.py:41
  (81 shorter events, 25.7 us)
Async XLA Ops:
  7.2 164.8 %copy-start = (bf16[128,128]{1,0:T(8,128)(2,1)S(1)}, bf16[128,128]{1,0:T(8,128)(2,1)}, u32[]{:S(2)}) copy-start(bf16[128,128]{1,0:T(8,128)(2,1)} %param.19) | copy-start | bytes 98308
  7.2 74.5 %all-gather.2.cloned.1.call-start = ((), (), s32[]{:S(2)}) async-start(), calls=%async_computation | async-start | bytes 11141120 | tf_op jit(solution)/shard_map/all_gather | solution.py:130
  10.1 42.7 %collective-permute-start = (bf16[320,1024]{1,0:T(8,128)(2,1)}, bf16[320,1024]{1,0:T(8,128)(2,1)}, u32[]{:S(2)}, u32[]{:S(2)}) collective-permute-start(bf16[320,1024]{1,0:T(8,128)(2,1)} %bitcast.50), channel_id=1, source_target_pairs={{0,32},{1,33},{2,34},{3,35},{4,36},{5,37},{6,38},{7,39},{8,40},{9,... | collective-permute-start | bytes 1966088 | tf_op jit(solution)/shard_map/ppermute | solution.py:41
  11.4 43.4 %collective-permute-start.1 = (bf16[320,1024]{1,0:T(8,128)(2,1)}, bf16[320,1024]{1,0:T(8,128)(2,1)}, u32[]{:S(2)}, u32[]{:S(2)}) collective-permute-start(bf16[320,1024]{1,0:T(8,128)(2,1)} %bitcast.51), channel_id=1, source_target_pairs={{0,96},{1,97},{2,98},{3,99},{4,100},{5,101},{6,102},{7,103},{8,104... | collective-permute-start | bytes 1966088 | tf_op jit(solution)/shard_map/ppermute | solution.py:41
  13.0 43.9 %collective-permute-start.2 = (bf16[320,1024]{1,0:T(8,128)(2,1)}, bf16[320,1024]{1,0:T(8,128)(2,1)S(1)}, u32[]{:S(2)}, u32[]{:S(2)}) collective-permute-start(bf16[320,1024]{1,0:T(8,128)(2,1)} %bitcast.52), channel_id=1, source_target_pairs={{0,64},{1,65},{2,66},{3,67},{4,68},{5,69},{6,70},{7,71},{8,72},{9,... | collective-permute-start | bytes 1966088 | tf_op jit(solution)/shard_map/ppermute | solution.py:41
  14.5 24.4 %collective-permute-start.3 = (bf16[320,1024]{1,0:T(8,128)(2,1)}, bf16[320,1024]{1,0:T(8,128)(2,1)S(1)}, u32[]{:S(2)}, u32[]{:S(2)}) collective-permute-start(bf16[320,1024]{1,0:T(8,128)(2,1)} %bitcast.53), channel_id=1, source_target_pairs={{0,16},{1,17},{2,18},{3,19},{4,20},{5,21},{6,22},{7,23},{8,24},{9,... | collective-permute-start | bytes 1966088 | tf_op jit(solution)/shard_map/ppermute | solution.py:41
  38.9 19.7 %collective-permute-start.4 = (bf16[320,1024]{1,0:T(8,128)(2,1)S(1)}, bf16[320,1024]{1,0:T(8,128)(2,1)S(1)}, u32[]{:S(2)}, u32[]{:S(2)}) collective-permute-start(bf16[320,1024]{1,0:T(8,128)(2,1)S(1)} %collective-permute-done.3), channel_id=1, source_target_pairs={{0,32},{1,33},{2,34},{3,35},{4,36},{5,37},{6,38},{7,39},{8,40},{9,... | collective-permute-start | bytes 1966088 | tf_op jit(solution)/shard_map/ppermute | solution.py:41
  38.9 20.6 %collective-permute-start.5 = (bf16[320,1024]{1,0:T(8,128)(2,1)S(1)}, bf16[320,1024]{1,0:T(8,128)(2,1)S(1)}, u32[]{:S(2)}, u32[]{:S(2)}) collective-permute-start(bf16[320,1024]{1,0:T(8,128)(2,1)S(1)} %collective-permute-done.3), channel_id=1, source_target_pairs={{0,96},{1,97},{2,98},{3,99},{4,100},{5,101},{6,102},{7,103},{8,104... | collective-permute-start | bytes 1966088 | tf_op jit(solution)/shard_map/ppermute | solution.py:41
  52.8 11.9 %collective-permute-start.6 = (bf16[320,1024]{1,0:T(8,128)(2,1)S(1)}, bf16[320,1024]{1,0:T(8,128)(2,1)S(1)}, u32[]{:S(2)}, u32[]{:S(2)}) collective-permute-start(bf16[320,1024]{1,0:T(8,128)(2,1)S(1)} %collective-permute-done.3), channel_id=1, source_target_pairs={{0,64},{1,65},{2,66},{3,67},{4,68},{5,69},{6,70},{7,71},{8,72},{9,... | collective-permute-start | bytes 1966088 | tf_op jit(solution)/shard_map/ppermute | solution.py:41
  81.7 17.1 %slice-start = ((s8[8388608]{0:T(1024)(128)(4,1)}), s8[4194304]{0:T(1024)(128)(4,1)S(1)}, s32[]{:S(2)}) async-start(s8[8388608]{0:T(1024)(128)(4,1)} %bitcast.37), calls=%async_computation.1 | async-start | bytes 8388608
  82.3 16.5 %slice-start.1 = ((s8[8388608]{0:T(1024)(128)(4,1)}), s8[4194304]{0:T(1024)(128)(4,1)S(1)}, s32[]{:S(2)}) async-start(s8[8388608]{0:T(1024)(128)(4,1)} %bitcast.37), calls=%async_computation.2 | async-start | bytes 8388608
  101.5 15.4 %collective-permute-start.9 = (bf16[256,1024]{1,0:T(8,128)(2,1)S(1)}, bf16[256,1024]{1,0:T(8,128)(2,1)S(1)}, u32[]{:S(2)}, u32[]{:S(2)}) collective-permute-start(bf16[256,1024]{1,0:T(8,128)(2,1)S(1)} %shard_map.128), channel_id=1, source_target_pairs={{0,32},{1,33},{2,34},{3,35},{4,36},{5,37},{6,38},{7,39},{8,40},{9,... | collective-permute-start | bytes 1572872 | tf_op jit(solution)/shard_map/ppermute | solution.py:41
  102.0 9.5 %collective-permute-start.7 = (bf16[256,512]{1,0:T(8,128)(2,1)S(1)}, bf16[256,512]{1,0:T(8,128)(2,1)S(1)}, u32[]{:S(2)}, u32[]{:S(2)}) collective-permute-start(bf16[256,512]{1,0:T(8,128)(2,1)S(1)} %shard_map.126), channel_id=1, source_target_pairs={{0,96},{1,97},{2,98},{3,99},{4,100},{5,101},{6,102},{7,103},{8,104... | collective-permute-start | bytes 786440 | tf_op jit(solution)/shard_map/ppermute | solution.py:41
  104.3 12.6 %collective-permute-start.8 = (bf16[256,512]{1,0:T(8,128)(2,1)S(1)}, bf16[256,512]{1,0:T(8,128)(2,1)S(1)}, u32[]{:S(2)}, u32[]{:S(2)}) collective-permute-start(bf16[256,512]{1,0:T(8,128)(2,1)S(1)} %shard_map.127), channel_id=1, source_target_pairs={{0,96},{1,97},{2,98},{3,99},{4,100},{5,101},{6,102},{7,103},{8,104... | collective-permute-start | bytes 786440 | tf_op jit(solution)/shard_map/ppermute | solution.py:41
  109.6 12.0 %collective-permute-start.10 = (bf16[256,512]{1,0:T(8,128)(2,1)S(1)}, bf16[256,512]{1,0:T(8,128)(2,1)S(1)}, u32[]{:S(2)}, u32[]{:S(2)}) collective-permute-start(bf16[256,512]{1,0:T(8,128)(2,1)S(1)} %shard_map.129), channel_id=1, source_target_pairs={{0,32},{1,33},{2,34},{3,35},{4,36},{5,37},{6,38},{7,39},{8,40},{9,... | collective-permute-start | bytes 786440 | tf_op jit(solution)/shard_map/ppermute | solution.py:41
  111.4 15.9 %collective-permute-start.13 = (bf16[256,512]{1,0:T(8,128)(2,1)S(1)}, bf16[256,512]{1,0:T(8,128)(2,1)S(1)}, u32[]{:S(2)}, u32[]{:S(2)}) collective-permute-start(bf16[256,512]{1,0:T(8,128)(2,1)S(1)} %shard_map.130), channel_id=1, source_target_pairs={{0,32},{1,33},{2,34},{3,35},{4,36},{5,37},{6,38},{7,39},{8,40},{9,... | collective-permute-start | bytes 786440 | tf_op jit(solution)/shard_map/ppermute | solution.py:41
  114.2 13.2 %collective-permute-start.15 = (bf16[256,512]{1,0:T(8,128)(2,1)S(1)}, bf16[256,512]{1,0:T(8,128)(2,1)S(1)}, u32[]{:S(2)}, u32[]{:S(2)}) collective-permute-start(bf16[256,512]{1,0:T(8,128)(2,1)S(1)} %add_convert_fusion.6), channel_id=1, source_target_pairs={{0,96},{1,97},{2,98},{3,99},{4,100},{5,101},{6,102},{7,103},{8,104... | collective-permute-start | bytes 786440 | tf_op jit(solution)/shard_map/ppermute | solution.py:41
  117.0 10.5 %collective-permute-start.16 = (bf16[256,512]{1,0:T(8,128)(2,1)S(1)}, bf16[256,512]{1,0:T(8,128)(2,1)S(1)}, u32[]{:S(2)}, u32[]{:S(2)}) collective-permute-start(bf16[256,512]{1,0:T(8,128)(2,1)S(1)} %add_convert_fusion.5), channel_id=1, source_target_pairs={{0,96},{1,97},{2,98},{3,99},{4,100},{5,101},{6,102},{7,103},{8,104... | collective-permute-start | bytes 786440 | tf_op jit(solution)/shard_map/ppermute | solution.py:41
  121.7 19.6 %collective-permute-start.11 = (bf16[256,1024]{1,0:T(8,128)(2,1)S(1)}, bf16[256,1024]{1,0:T(8,128)(2,1)S(1)}, u32[]{:S(2)}, u32[]{:S(2)}) collective-permute-start(bf16[256,1024]{1,0:T(8,128)(2,1)S(1)} %get-tuple-element.49), channel_id=1, source_target_pairs={{0,96},{1,97},{2,98},{3,99},{4,100},{5,101},{6,102},{7,103},{8,104... | collective-permute-start | bytes 1572872 | tf_op jit(solution)/shard_map/ppermute | solution.py:41
  127.7 13.6 %collective-permute-start.17 = (bf16[256,1024]{1,0:T(8,128)(2,1)S(1)}, bf16[256,1024]{1,0:T(8,128)(2,1)S(1)}, u32[]{:S(2)}, u32[]{:S(2)}) collective-permute-start(bf16[256,1024]{1,0:T(8,128)(2,1)S(1)} %add_convert_fusion), channel_id=1, source_target_pairs={{0,16},{1,17},{2,18},{3,19},{4,20},{5,21},{6,22},{7,23},{8,24},{9,... | collective-permute-start | bytes 1572872 | tf_op jit(solution)/shard_map/ppermute | solution.py:41
  131.1 6.7 %collective-permute-start.12 = (bf16[256,512]{1,0:T(8,128)(2,1)S(1)}, bf16[256,512]{1,0:T(8,128)(2,1)S(1)}, u32[]{:S(2)}, u32[]{:S(2)}) collective-permute-start(bf16[256,512]{1,0:T(8,128)(2,1)S(1)} %get-tuple-element.61), channel_id=1, source_target_pairs={{0,32},{1,33},{2,34},{3,35},{4,36},{5,37},{6,38},{7,39},{8,40},{9,... | collective-permute-start | bytes 786440 | tf_op jit(solution)/shard_map/ppermute | solution.py:41
  131.1 10.1 %collective-permute-start.14 = (bf16[256,512]{1,0:T(8,128)(2,1)S(1)}, bf16[256,512]{1,0:T(8,128)(2,1)S(1)}, u32[]{:S(2)}, u32[]{:S(2)}) collective-permute-start(bf16[256,512]{1,0:T(8,128)(2,1)S(1)} %get-tuple-element.60), channel_id=1, source_target_pairs={{0,32},{1,33},{2,34},{3,35},{4,36},{5,37},{6,38},{7,39},{8,40},{9,... | collective-permute-start | bytes 786440 | tf_op jit(solution)/shard_map/ppermute | solution.py:41
  141.7 19.1 %collective-permute-start.18 = (bf16[128,1024]{1,0:T(8,128)(2,1)S(1)}, bf16[128,1024]{1,0:T(8,128)(2,1)S(1)}, u32[]{:S(2)}, u32[]{:S(2)}) collective-permute-start(bf16[128,1024]{1,0:T(8,128)(2,1)S(1)} %get-tuple-element.58), channel_id=1, source_target_pairs={{0,6},{1,7},{2,18},{3,27},{4,36},{5,43},{6,48},{7,57},{8,72},{9,75... | collective-permute-start | bytes 786440 | tf_op jit(solution)/shard_map/ppermute | solution.py:41
  141.7 30.2 %collective-permute-start.19 = (bf16[128,1024]{1,0:T(8,128)(2,1)S(1)}, bf16[128,1024]{1,0:T(8,128)(2,1)S(1)}, u32[]{:S(2)}, u32[]{:S(2)}) collective-permute-start(bf16[128,1024]{1,0:T(8,128)(2,1)S(1)} %get-tuple-element.59), channel_id=1, source_target_pairs={{0,7},{1,6},{2,19},{3,26},{4,37},{5,42},{6,49},{7,56},{8,73},{9,74... | collective-permute-start | bytes 786440 | tf_op jit(solution)/shard_map/ppermute | solution.py:41
  (6 other events, 69.4 us)
Sparse Core Ops, SparseCore 0:
  10.3 71.3 all-gather.1
